TPU v7x, 512 devices: a whole 4x4x16 slice. The times are simulated.
512 devices in a mesh: fsdp: 64 (over y, z), rep: 8 (over x, core).
Axes of the slice: x: 4, y: 4, z: 16, core: 2. Of those that a mesh axis runs over, the one named last changes fastest.
Arguments:
- grads: bfloat16 [512, 512, 512], P('rep', 'fsdp'), may hold values from -8 to 8
- left_state: bfloat16 [1024, 512, 512], P(('fsdp', 'rep')), may hold values from -1.203125 to 120
- right_state: bfloat16 [1024, 512, 512], P(('fsdp', 'rep')), may hold values from -1.203125 to 120
- block_owner: int32 [512], replicated, may hold values from 0 to 1023, as said below
Outputs:
- update: bfloat16 [512, 512, 512], P('rep', 'fsdp')
- left_new: bfloat16 [1024, 512, 512], P(('fsdp', 'rep'))
- right_new: bfloat16 [1024, 512, 512], P(('fsdp', 'rep'))
Inputs may be any that keep to these rules, and one draw needn't show every extreme that they name: `block_owner`: each entry is a slot number: the device's index along fsdp+rep (fsdp index times 8 plus rep index) times 2 plus the slot on that device. No two blocks share a slot. Block b is held by rep index b // 64; for every pair of rep indices g and c exactly 8 of the blocks held by g are owned by devices of rep index c. A device owns 0, 1 or 2 blocks, and in every draw some device owns 2. Where the device at fsdp index f owns two blocks, the device at fsdp index f XOR 64 / 2 with the same rep index owns none.
All inputs are finite; a program needn't handle non-finite values.
Results may differ from a plain program's by a relative error of at most 0.0086.
Values may be sent and summed in bfloat16 or wider, within the bound.
No kernel may reach another device: no remote copies, remote signals or barrier semaphores. Data moves between devices by JAX's collectives and lax.ppermute only.
A program may use at most 64 MiB of HBM per device.

v0:
```python
import jax
import jax.numpy as jnp
from jax import lax
from jax.sharding import PartitionSpec as P

ITERS = 2


DECAY_RATE = 0.95


def multiply(first, second):
    return jnp.dot(first, second, preferred_element_type=jnp.float32)


def inverse_root(stored):
    factor = stored.astype(jnp.float32)
    scaling = 2.5 / jnp.sqrt(jnp.sum(factor * factor))
    current = scaling * factor
    identity = jnp.eye(factor.shape[0], dtype=jnp.float32)
    result = current.astype(jnp.bfloat16)
    for iteration in range(ITERS):
        tangent = ((5.0 * identity - current) * 0.25).astype(jnp.bfloat16)
        if iteration == 0:
            result = tangent
        else:
            result = multiply(result, tangent).astype(jnp.bfloat16)
        if iteration + 1 < ITERS:
            square = multiply(tangent, tangent).astype(jnp.bfloat16)
            fourth = multiply(square, square).astype(jnp.bfloat16)
            current = multiply(fourth, current.astype(jnp.bfloat16))
    return result


def refresh(old_left, old_right, gradient):
    left_gram = lax.dot_general(
        gradient, gradient, (((1,), (1,)), ((), ())), preferred_element_type=jnp.float32
    )
    right_gram = lax.dot_general(
        gradient, gradient, (((0,), (0,)), ((), ())), preferred_element_type=jnp.float32
    )
    left_factor = (
        DECAY_RATE * old_left.astype(jnp.float32) + (1.0 - DECAY_RATE) * left_gram
    ).astype(jnp.bfloat16)
    right_factor = (
        DECAY_RATE * old_right.astype(jnp.float32) + (1.0 - DECAY_RATE) * right_gram
    ).astype(jnp.bfloat16)
    return (left_factor, right_factor)


def keep_factors(old_left, old_right, gradient):
    return (old_left, old_right)


def precondition(left_factor, right_factor, gradient):
    half_product = multiply(inverse_root(left_factor), gradient).astype(jnp.bfloat16)
    raw_update = multiply(half_product, inverse_root(right_factor))
    wide = gradient.astype(jnp.float32)
    grad_norm = jnp.sqrt(jnp.sum(wide * wide))
    raw_norm = jnp.sqrt(jnp.sum(raw_update * raw_update))
    return (raw_update * (grad_norm / (raw_norm + 1e-06))).astype(jnp.bfloat16)


def blank_update(left_factor, right_factor, gradient):
    return jnp.zeros(gradient.shape, jnp.bfloat16)


def slots_owned(block_owner, first_slot, slot_count):
    wanted = first_slot + jnp.arange(slot_count, dtype=jnp.int32)
    return jnp.any(block_owner[None, :] == wanted[:, None], axis=1)


def local(grads, left_state, right_state, block_owner):
    rep_count = lax.axis_size("rep")
    fsdp_count = lax.axis_size("fsdp")
    group_index = lax.axis_index("rep")
    place_index = lax.axis_index("fsdp")
    held_blocks, shard_rows, block_width = grads.shape
    column_share = held_blocks // rep_count
    slot_count = left_state.shape[0]
    owner_table = block_owner.reshape(rep_count, held_blocks)
    owner_column = owner_table // slot_count % rep_count
    positions = jnp.arange(held_blocks, dtype=jnp.int32)
    earlier = (owner_column[:, :, None] == owner_column[:, None, :]) & (
        positions[None, None, :] < positions[None, :, None]
    )
    ranking = jnp.sum(earlier.astype(jnp.int32), axis=2)
    send_order = owner_column * column_share + ranking
    matches = send_order[:, None, :] == positions[None, :, None]
    picked = jnp.sum(jnp.where(matches, positions[None, None, :], 0), axis=2)
    my_picked = lax.dynamic_index_in_dim(picked, group_index, 0, keepdims=False)
    my_order = lax.dynamic_index_in_dim(send_order, group_index, 0, keepdims=False)
    entry_local = lax.dynamic_slice_in_dim(picked, group_index * column_share, column_share, 1)
    entry_global = (
        jnp.arange(rep_count, dtype=jnp.int32)[:, None] * held_blocks + entry_local
    ).reshape(-1)
    outgoing = jnp.take(grads, my_picked, axis=0)
    arrived = lax.all_to_all(outgoing, "rep", split_axis=0, concat_axis=0, tiled=True)
    entry_owner = jnp.take(block_owner, entry_global)
    destination = entry_owner // slot_count // rep_count * slot_count + entry_owner % slot_count
    spots = jnp.arange(fsdp_count * slot_count, dtype=jnp.int32)
    hits = destination[None, :] == spots[:, None]
    source_entry = jnp.sum(jnp.where(hits, positions[None, :], 0), axis=1)
    filled = jnp.any(hits, axis=1)
    packed = jnp.where(
        filled[:, None, None], jnp.take(arrived, source_entry, axis=0), jnp.zeros((), jnp.bfloat16)
    )
    packed = packed.reshape(fsdp_count, slot_count, shard_rows, block_width)
    whole_blocks = lax.all_to_all(packed, "fsdp", split_axis=0, concat_axis=2, tiled=True)[0]
    first_slot = (place_index * rep_count + group_index) * slot_count
    owned = slots_owned(block_owner, first_slot, slot_count)
    left_parts = []
    right_parts = []
    for slot_number in range(slot_count):
        left_factor, right_factor = lax.cond(
            owned[slot_number],
            refresh,
            keep_factors,
            left_state[slot_number],
            right_state[slot_number],
            whole_blocks[slot_number],
        )
        left_parts.append(left_factor)
        right_parts.append(right_factor)
    left_new = jnp.stack(left_parts)
    right_new = jnp.stack(right_parts)
    updates = jnp.stack(
        [
            lax.cond(
                owned[slot_number],
                precondition,
                blank_update,
                left_new[slot_number],
                right_new[slot_number],
                whole_blocks[slot_number],
            )
            for slot_number in range(slot_count)
        ]
    )
    returned_rows = lax.all_to_all(updates[None], "fsdp", split_axis=2, concat_axis=0, tiled=True)
    flat_rows = returned_rows.reshape(fsdp_count * slot_count, shard_rows, block_width)
    home_entries = jnp.take(flat_rows, destination, axis=0)
    at_home = lax.all_to_all(home_entries, "rep", split_axis=0, concat_axis=0, tiled=True)
    update = jnp.take(at_home, my_order, axis=0)
    return (update, left_new, right_new)


def solution(mesh):
    return jax.shard_map(
        local,
        mesh=mesh,
        in_specs=(
            P("rep", "fsdp", None),
            P(("fsdp", "rep"), None, None),
            P(("fsdp", "rep"), None, None),
            P(),
        ),
        out_specs=(
            P("rep", "fsdp", None),
            P(("fsdp", "rep"), None, None),
            P(("fsdp", "rep"), None, None),
        ),
        check_vma=False,
    )
```

profile of v0, /device:TPU:1, one launch (start us, length us, event | category | flops | bytes accessed | tf_op | source)
XLA Modules:
  0.0 218.6 jit_solution(15064476123558214811)
XLA Ops:
  5.4 10.3 %all-to-all-start = ((bf16[64,8,512]{2,1,0:T(8,128)(2,1)}), bf16[64,8,512]{2,1,0:T(8,128)(2,1)S(1)}, u32[]{:S(2)}, u32[]{:S(2)}) async-start(bf16[64,8,512]{2,1,0:T(8,128)(2,1)} %broadcast_select_fusion.1), calls=%async_computation | async-start | bytes 1048576 | tf_op jit(solution)/shard_map/all_to_all | solution.py:98
  16.2 9.0 %all-to-all-done = bf16[64,8,512]{2,1,0:T(8,128)(2,1)S(1)} async-done(((bf16[64,8,512]{2,1,0:T(8,128)(2,1)}), bf16[64,8,512]{2,1,0:T(8,128)(2,1)S(1)}, u32[]{:S(2)}, u32[]{:S(2)}) %all-to-all-start) | async-done | bytes 524320 | tf_op jit(solution)/shard_map/all_to_all | solution.py:98
  27.1 14.4 %all-to-all-start.1 = ((bf16[64,2,8,512]{3,2,1,0:T(8,128)(2,1)}), bf16[64,2,8,512]{3,2,1,0:T(8,128)(2,1)}, u32[]{:S(2)}, u32[]{:S(2)}) async-start(bf16[64,2,8,512]{3,2,1,0:T(8,128)(2,1)} %select_select_fusion), calls=%async_computation.1 | async-start | bytes 2097152 | tf_op jit(solution)/shard_map/all_to_all | solution.py:109
  43.5 1.7 slice_bitcast_fusion.4
  45.2 46.4 %all-to-all-done.1 = bf16[64,2,8,512]{3,2,1,0:T(8,128)(2,1)} async-done(((bf16[64,2,8,512]{3,2,1,0:T(8,128)(2,1)}), bf16[64,2,8,512]{3,2,1,0:T(8,128)(2,1)}, u32[]{:S(2)}, u32[]{:S(2)}) %all-to-all-start.1) | async-done | bytes 1048608 | tf_op jit(solution)/shard_map/all_to_all | solution.py:109
  93.7 2.7 %conditional.6 = (bf16[512,512]{1,0:T(8,128)(2,1)S(1)}, bf16[512,512]{1,0:T(8,128)(2,1)S(1)}, bf16[1,512,512]{2,1,0:T(8,128)(2,1)}, bf16[1,512,512]{2,1,0:T(8,128)(2,1)}) conditional(s32[]{:T(128)} %bitcast.22, (bf16[512,512]{1,0:T(8,128)(2,1)S(1)}, bf16[512,512]{1,0:T(8,128)(2,1)S(1)}) %tuple.72, (bf16[512,512]{1,0:T(8,128)(2,1)S(1)}, ...), branch_computations={%region_13.15_spmd, %region_14.16_spmd} | conditional | flops 539492352 | bytes 5242912 | solution.py:115
  96.4 20.6 %conditional.7 = (bf16[1,512,512]{2,0,1:T(2,128)(2,1)}) conditional(s32[]{:T(128)} %bitcast.22, () %tuple.71, (bf16[512,512]{1,0:T(8,128)(2,1)S(1)}, bf16[512,512]{1,0:T(8,128)(2,1)}, bf16[512,512]{1,0:T(8,128)(2,1)S(1)}) %tuple.111), branch_computations={%region_15.17_spmd, %region_16.22_spmd} | conditional | flops 2701131776 | bytes 14155928 | solution.py:129
  98.0 1.9 convolution_convert_fusion.8
  99.9 2.6 %convolution_convert_fusion.7 = bf16[512,512]{1,0:T(8,128)(2,1)} fusion(bf16[512,512]{1,0:T(8,128)(2,1)} %convolution_convert_fusion.8, bf16[512,512]{1,0:T(8,128)(2,1)S(1)} %get-tuple-element.76, f32[]{:T(128)S(6)} %div.26), kind=kOutput, calls=%fused_computation.80 | convolution fusion | flops 541065216 | bytes 1572868 | tf_op jit(solution)/shard_map/cond/branch_1_fun/dot_general | solution.py:13
  103.3 1.9 convolution_convert_fusion.12
  105.2 2.7 %convolution_convert_fusion.11 = bf16[512,512]{1,0:T(8,128)(2,1)} fusion(bf16[512,512]{1,0:T(8,128)(2,1)} %convolution_convert_fusion.12, bf16[512,512]{1,0:T(8,128)(2,1)S(1)} %get-tuple-element.74, f32[]{:T(128)S(6)} %div.25), kind=kOutput, calls=%fused_computation.84 | convolution fusion | flops 541065216 | bytes 1572868 | tf_op jit(solution)/shard_map/cond/branch_1_fun/dot_general | solution.py:13
  108.0 3.5 %multiply_reduce_fusion.2 = (f32[]{:T(128)}, f32[512,512]{1,0:T(8,128)}) fusion(bf16[512,512]{1,0:T(8,128)(2,1)} %convolution_convert_fusion.7, bf16[512,512]{1,0:T(8,128)(2,1)} %convolution_convert_fusion.11, bf16[512,512]{1,0:T(8,128)(2,1)S(1)} %copy-done.3), kind=kOutput, calls=%fused_computation.99 | convolution fusion | flops 537657344 | bytes 2621444 | tf_op jit(solution)/shard_map/cond/branch_1_fun/dot_general | solution.py:13
  115.2 1.8 copy.28
  118.2 15.9 %conditional.5 = (bf16[1,512,512]{2,0,1:T(2,128)(2,1)S(1)}) conditional(s32[]{:T(128)} %bitcast.12, () %tuple.67, (bf16[512,512]{1,0:T(8,128)(2,1)S(1)}, bf16[512,512]{1,0:T(8,128)(2,1)S(1)}, bf16[512,512]{1,0:T(8,128)(2,1)S(1)}) %tuple.70), branch_computations={%region_7.9_spmd, %region_8.14_spmd} | conditional | flops 2701131776 | bytes 12058748 | solution.py:129
  120.0 1.9 convolution_convert_fusion.1
  121.9 2.6 %convolution_convert_fusion = bf16[512,512]{1,0:T(8,128)(2,1)} fusion(bf16[512,512]{1,0:T(8,128)(2,1)} %convolution_convert_fusion.1, bf16[512,512]{1,0:T(8,128)(2,1)S(1)} %get-tuple-element.70, f32[]{:T(128)S(6)} %div.23), kind=kOutput, calls=%fused_computation.21 | convolution fusion | flops 541065216 | bytes 1572868 | tf_op jit(solution)/shard_map/cond/branch_1_fun/dot_general | solution.py:13
  128.1 2.7 %multiply_reduce_fusion = (f32[]{:T(128)}, f32[512,512]{1,0:T(8,128)S(1)}) fusion(bf16[512,512]{1,0:T(8,128)(2,1)} %convolution_convert_fusion, bf16[512,512]{1,0:T(8,128)(2,1)} %convolution_convert_fusion.4, bf16[512,512]{1,0:T(8,128)(2,1)S(1)} %get-tuple-element.69), kind=kOutput, calls=%fused_computation.40 | convolution fusion | flops 537657344 | bytes 2621444 | tf_op jit(solution)/shard_map/cond/branch_1_fun/dot_general | solution.py:13
  134.1 4.2 %maximum_bitcast_fusion = bf16[1,2,512,512]{3,1,0,2:T(2,128)(2,1)} fusion(bf16[1,512,512]{2,0,1:T(2,128)(2,1)} %get-tuple-element.97, bf16[1,512,512]{2,0,1:T(2,128)(2,1)S(1)} %get-tuple-element.96), kind=kLoop, calls=%fused_computation.123 | loop fusion | flops 2097152 | bytes 2097152 | tf_op jit(solution)/shard_map/broadcast_in_dim | solution.py:140
  138.3 8.9 %all-to-all-start.2 = ((bf16[1,2,512,512]{3,1,0,2:T(2,128)(2,1)}), bf16[1,2,512,512]{3,1,0,2:T(2,128)(2,1)S(1)}, u32[]{:S(2)}, u32[]{:S(2)}) async-start(bf16[1,2,512,512]{3,1,0,2:T(2,128)(2,1)} %maximum_bitcast_fusion), calls=%async_computation.2 | async-start | bytes 2097152 | tf_op jit(solution)/shard_map/all_to_all | solution.py:140
  147.3 48.5 %all-to-all-done.2 = bf16[1,2,512,512]{3,1,0,2:T(2,128)(2,1)S(1)} async-done(((bf16[1,2,512,512]{3,1,0,2:T(2,128)(2,1)}), bf16[1,2,512,512]{3,1,0,2:T(2,128)(2,1)S(1)}, u32[]{:S(2)}, u32[]{:S(2)}) %all-to-all-start.2) | async-done | bytes 1048608 | tf_op jit(solution)/shard_map/all_to_all | solution.py:140
  197.6 9.9 %all-to-all-start.3 = ((bf16[64,8,512]{2,1,0:T(8,128)(2,1)}), bf16[64,8,512]{2,1,0:T(8,128)(2,1)S(1)}, u32[]{:S(2)}, u32[]{:S(2)}) async-start(bf16[64,8,512]{2,1,0:T(8,128)(2,1)} %broadcast_select_fusion.2), calls=%async_computation.3 | async-start | bytes 1048576 | tf_op jit(solution)/shard_map/all_to_all | solution.py:143
  207.6 2.1 pad_maximum_fusion
  209.7 2.1 pad_maximum_fusion.1
  211.8 5.2 %all-to-all-done.3 = bf16[64,8,512]{2,1,0:T(8,128)(2,1)S(1)} async-done(((bf16[64,8,512]{2,1,0:T(8,128)(2,1)}), bf16[64,8,512]{2,1,0:T(8,128)(2,1)S(1)}, u32[]{:S(2)}, u32[]{:S(2)}) %all-to-all-start.3) | async-done | bytes 524320 | tf_op jit(solution)/shard_map/all_to_all | solution.py:143
  (66 shorter events, 27.1 us)
Async XLA Ops:
  0.6 3.2 %copy-start = (bf16[64,8,512]{2,1,0:T(8,128)(2,1)S(1)}, bf16[64,8,512]{2,1,0:T(8,128)(2,1)}, u32[]{:S(2)}) copy-start(bf16[64,8,512]{2,1,0:T(8,128)(2,1)} %param.14) | copy-start | bytes 1572868
  5.4 19.8 %all-to-all-start = ((bf16[64,8,512]{2,1,0:T(8,128)(2,1)}), bf16[64,8,512]{2,1,0:T(8,128)(2,1)S(1)}, u32[]{:S(2)}, u32[]{:S(2)}) async-start(bf16[64,8,512]{2,1,0:T(8,128)(2,1)} %broadcast_select_fusion.1), calls=%async_computation | async-start | bytes 1048576 | tf_op jit(solution)/shard_map/all_to_all | solution.py:98
  27.1 14.4 %copy-start.1 = (s32[512]{0:T(512)S(1)}, s32[512]{0:T(512)}, u32[]{:S(2)}) copy-start(s32[512]{0:T(512)} %param.17) | copy-start | bytes 6148
  27.1 64.5 %all-to-all-start.1 = ((bf16[64,2,8,512]{3,2,1,0:T(8,128)(2,1)}), bf16[64,2,8,512]{3,2,1,0:T(8,128)(2,1)}, u32[]{:S(2)}, u32[]{:S(2)}) async-start(bf16[64,2,8,512]{3,2,1,0:T(8,128)(2,1)} %select_select_fusion), calls=%async_computation.1 | async-start | bytes 2097152 | tf_op jit(solution)/shard_map/all_to_all | solution.py:109
  92.9 0.8 copy-start.2
  105.2 2.7 %copy-start.3 = (bf16[512,512]{1,0:T(8,128)(2,1)S(1)}, bf16[512,512]{1,0:T(8,128)(2,1)}, u32[]{:S(2)}) copy-start(bf16[512,512]{1,0:T(8,128)(2,1)} %get-tuple-element.75) | copy-start | bytes 1572868 | tf_op jit(solution)/shard_map/cond
  138.3 57.4 %all-to-all-start.2 = ((bf16[1,2,512,512]{3,1,0,2:T(2,128)(2,1)}), bf16[1,2,512,512]{3,1,0,2:T(2,128)(2,1)S(1)}, u32[]{:S(2)}, u32[]{:S(2)}) async-start(bf16[1,2,512,512]{3,1,0,2:T(2,128)(2,1)} %maximum_bitcast_fusion), calls=%async_computation.2 | async-start | bytes 2097152 | tf_op jit(solution)/shard_map/all_to_all | solution.py:140
  197.6 19.4 %all-to-all-start.3 = ((bf16[64,8,512]{2,1,0:T(8,128)(2,1)}), bf16[64,8,512]{2,1,0:T(8,128)(2,1)S(1)}, u32[]{:S(2)}, u32[]{:S(2)}) async-start(bf16[64,8,512]{2,1,0:T(8,128)(2,1)} %broadcast_select_fusion.2), calls=%async_computation.3 | async-start | bytes 1048576 | tf_op jit(solution)/shard_map/all_to_all | solution.py:143
where the time goes:
time: 220 us; the launch traced here: 219 us
  waiting for transfers between devices  109 us (50%)
  starting transfers between devices  43.5 us (20%)
  matrix products  24.9 us (11%)
  other arithmetic  18.8 us (9%)
  local copies, waits for them, and re-layouts  14.1 us (6%)
  loops' own time  6.04 us (3%)
    all_to_all x1, waiting for transfers between devices, local(): lax.all_to_all(updates[None], 'fsdp', split_axis=2, concat_axis=0, tiled=...  48.5 us
    all_to_all x1, waiting for transfers between devices, local(): lax.all_to_all(packed, 'fsdp', split_axis=0, concat_axis=2, tiled=True)[0]  46.4 us
    dot_general x10, matrix products, multiply(): return jnp.dot(first, second, preferred_element_type=jnp.float32)  22.7 us
    all_to_all x1, starting transfers between devices, local(): lax.all_to_all(packed, 'fsdp', split_axis=0, concat_axis=2, tiled=True)[0]  14.4 us
    all_to_all x1, starting transfers between devices, local(): lax.all_to_all(outgoing, 'rep', split_axis=0, concat_axis=0, tiled=True)  10.3 us
    all_to_all x1, starting transfers between devices, local(): lax.all_to_all(home_entries, 'rep', split_axis=0, concat_axis=0, tiled=True)  9.93 us
    all_to_all x1, waiting for transfers between devices, local(): lax.all_to_all(outgoing, 'rep', split_axis=0, concat_axis=0, tiled=True)  8.97 us
    all_to_all x1, starting transfers between devices, local(): lax.all_to_all(updates[None], 'fsdp', split_axis=2, concat_axis=0, tiled=...  8.93 us
  transfers between devices with their start and end apart: 4, of which 4 were waited for; matrix products, arithmetic and copies ran while one was open for 3% of the time, Pallas kernels for 0%

commit v1 on v0

v1 whole, which is shorter than its diff:
```python
import jax
import jax.numpy as jnp
from jax import lax
from jax.experimental import pallas as pl
from jax.experimental.pallas import tpu as pltpu
from jax.sharding import PartitionSpec as P

ITERS = 2
DECAY_RATE = 0.95
VMEM_LIMIT = 32 * 1024 * 1024


def multiply(first, second):
    return jnp.dot(first, second, preferred_element_type=jnp.float32)


def inverse_root(stored):
    factor = stored.astype(jnp.float32)
    scaling = 2.5 / jnp.sqrt(jnp.sum(factor * factor))
    current = scaling * factor
    width = factor.shape[0]
    rows = lax.broadcasted_iota(jnp.int32, (width, width), 0)
    columns = lax.broadcasted_iota(jnp.int32, (width, width), 1)
    five = jnp.where(rows == columns, 5.0, 0.0)
    result = None
    for iteration in range(ITERS):
        tangent = ((five - current) * 0.25).astype(jnp.bfloat16)
        if iteration == 0:
            result = tangent
        else:
            result = multiply(result, tangent).astype(jnp.bfloat16)
        if iteration + 1 < ITERS:
            square = multiply(tangent, tangent).astype(jnp.bfloat16)
            fourth = multiply(square, square).astype(jnp.bfloat16)
            current = multiply(fourth, current.astype(jnp.bfloat16))
    return result


def block_kernel(
    choice, gradient_ref, left_own, right_own, left_lent, right_lent,
    update_ref, left_ref, right_ref, left_old, right_old, sems,
):
    lent, slot = choice[0], choice[1]

    @pl.when(lent == 1)
    def _():
        pltpu.make_async_copy(left_lent, left_old, sems.at[0]).start()
        pltpu.make_async_copy(right_lent, right_old, sems.at[1]).start()

    @pl.when(lent == 0)
    def _():
        pltpu.make_async_copy(left_own.at[slot], left_old, sems.at[0]).start()
        pltpu.make_async_copy(right_own.at[slot], right_old, sems.at[1]).start()

    pltpu.make_async_copy(left_lent, left_old, sems.at[0]).wait()
    pltpu.make_async_copy(right_lent, right_old, sems.at[1]).wait()
    gradient = gradient_ref[...]
    left_gram = lax.dot_general(
        gradient, gradient, (((1,), (1,)), ((), ())), preferred_element_type=jnp.float32
    )
    left_factor = (
        DECAY_RATE * left_old[...].astype(jnp.float32) + (1.0 - DECAY_RATE) * left_gram
    ).astype(jnp.bfloat16)
    left_ref[...] = left_factor
    right_gram = lax.dot_general(
        gradient, gradient, (((0,), (0,)), ((), ())), preferred_element_type=jnp.float32
    )
    right_factor = (
        DECAY_RATE * right_old[...].astype(jnp.float32) + (1.0 - DECAY_RATE) * right_gram
    ).astype(jnp.bfloat16)
    right_ref[...] = right_factor
    left_root = inverse_root(left_factor)
    right_root = inverse_root(right_factor)
    half_product = multiply(left_root, gradient).astype(jnp.bfloat16)
    raw_update = multiply(half_product, right_root)
    wide = gradient.astype(jnp.float32)
    grad_norm = jnp.sqrt(jnp.sum(wide * wide))
    raw_norm = jnp.sqrt(jnp.sum(raw_update * raw_update))
    update_ref[...] = (raw_update * (grad_norm / (raw_norm + 1e-06))).astype(jnp.bfloat16)


def work_on_block(choice, gradient, left_state, right_state, left_lent, right_lent):
    width = gradient.shape[0]
    square = jax.ShapeDtypeStruct((width, width), jnp.bfloat16)
    return pl.pallas_call(
        block_kernel,
        out_shape=(square, square, square),
        in_specs=[
            pl.BlockSpec(memory_space=pltpu.SMEM),
            pl.BlockSpec(memory_space=pltpu.VMEM),
        ]
        + [pl.BlockSpec(memory_space=pl.ANY)] * 4,
        out_specs=[pl.BlockSpec(memory_space=pltpu.VMEM)] * 3,
        scratch_shapes=[
            pltpu.VMEM((width, width), jnp.bfloat16),
            pltpu.VMEM((width, width), jnp.bfloat16),
            pltpu.SemaphoreType.DMA((2,)),
        ],
        compiler_params=pltpu.CompilerParams(vmem_limit_bytes=VMEM_LIMIT),
        cost_estimate=pl.CostEstimate(
            flops=24 * width**3, bytes_accessed=12 * width**2, transcendentals=0
        ),
        name="block_step",
    )(choice, gradient, left_state, right_state, left_lent, right_lent)


def pick(array, order):
    return array.at[order].get(mode="promise_in_bounds", unique_indices=True)


def local(grads, left_state, right_state, block_owner):
    rep_count = lax.axis_size("rep")
    fsdp_count = lax.axis_size("fsdp")
    group_index = lax.axis_index("rep")
    place_index = lax.axis_index("fsdp")
    held_blocks, shard_rows, block_width = grads.shape
    column_share = held_blocks // rep_count
    slot_count = left_state.shape[0]
    half = fsdp_count // 2
    swap = [(place, place ^ half) for place in range(fsdp_count)]
    positions = jnp.arange(held_blocks, dtype=jnp.int32)

    left_lent = lax.ppermute(left_state[1], "fsdp", swap)
    right_lent = lax.ppermute(right_state[1], "fsdp", swap)

    owner_table = block_owner.reshape(rep_count, held_blocks)
    owner_column = owner_table // slot_count % rep_count
    before = positions[None, :] < positions[:, None]

    my_column = lax.dynamic_index_in_dim(owner_column, group_index, 0, keepdims=False)
    alike = (my_column[:, None] == my_column[None, :]) & before
    my_order = my_column * column_share + jnp.sum(alike.astype(jnp.int32), axis=1)
    my_picked = jnp.sum(
        jnp.where(my_order[None, :] == positions[:, None], positions[None, :], 0), axis=1
    )
    arrived = lax.all_to_all(
        pick(grads, my_picked), "rep", split_axis=0, concat_axis=0, tiled=True
    )

    mine = owner_column == group_index
    rank = jnp.sum((mine[:, None, :] & before[None]).astype(jnp.int32), axis=2)
    shares = jnp.arange(column_share, dtype=jnp.int32)
    taken = mine[:, None, :] & (rank[:, None, :] == shares[None, :, None])
    entry_owner = jnp.sum(jnp.where(taken, owner_table[:, None, :], 0), axis=2).reshape(-1)

    sibling = jnp.any(entry_owner[None, :] == entry_owner[:, None] - 1, axis=1)
    second = (entry_owner % slot_count == 1) & sibling
    owner_place = entry_owner // (slot_count * rep_count)
    worker = jnp.where(second, owner_place ^ half, owner_place)
    source_entry = jnp.sum(
        jnp.where(worker[None, :] == positions[:, None], positions[None, :], 0), axis=1
    )
    gradient = lax.all_to_all(
        pick(arrived, source_entry), "fsdp", split_axis=0, concat_axis=0, tiled=True
    ).reshape(fsdp_count * shard_rows, block_width)

    first_slot = (place_index * rep_count + group_index) * slot_count
    owns_first = jnp.any(entry_owner == first_slot)
    owns_second = jnp.any(entry_owner == first_slot + 1)
    lent = ~(owns_first | owns_second)
    choice = jnp.stack([lent, ~owns_first]).astype(jnp.int32)
    update_block, left_done, right_done = work_on_block(
        choice, gradient, left_state, right_state, left_lent, right_lent
    )

    returned_rows = lax.all_to_all(
        update_block.reshape(fsdp_count, shard_rows, block_width),
        "fsdp", split_axis=0, concat_axis=0, tiled=True,
    )
    left_back = lax.ppermute(left_done, "fsdp", swap)
    right_back = lax.ppermute(right_done, "fsdp", swap)
    at_home = lax.all_to_all(
        pick(returned_rows, worker), "rep", split_axis=0, concat_axis=0, tiled=True
    )
    update = pick(at_home, my_order)

    def settled(state, done, back):
        first = jnp.where(owns_first, done, state[0])
        other = jnp.where(owns_first, back, done)
        return jnp.stack([first, jnp.where(owns_second, other, state[1])])

    return (
        update,
        settled(left_state, left_done, left_back),
        settled(right_state, right_done, right_back),
    )


def solution(mesh):
    return jax.shard_map(
        local,
        mesh=mesh,
        in_specs=(
            P("rep", "fsdp", None),
            P(("fsdp", "rep"), None, None),
            P(("fsdp", "rep"), None, None),
            P(),
        ),
        out_specs=(
            P("rep", "fsdp", None),
            P(("fsdp", "rep"), None, None),
            P(("fsdp", "rep"), None, None),
        ),
        check_vma=False,
    )
```

time: 220 us -> 144 us (0.65)
  waiting for transfers between devices: 109 us -> 53.4 us
  matrix products: 24.9 us -> 0 us
  starting transfers between devices: 43.5 us -> 59.4 us
  other arithmetic: 18.8 us -> 9.63 us
  Pallas kernels: 0 us -> 6.52 us
  loops' own time: 6.04 us -> 0 us
  local copies, waits for them, and re-layouts: 14.1 us -> 11.6 us
    all_to_all x4, waiting for transfers between devices: 109 us -> 20.1 us  [the longest x1 8.6 us: local(): lax.all_to_all(pick(grads, my_picked), 'rep', split_axis=0, concat_axis=0...]
    ppermute x0 -> x4, waiting for transfers between devices: none -> 33.2 us  [the longest x1 13.5 us: local(): left_lent = lax.ppermute(left_state[1], 'fsdp', swap)]
    dot_general x14 -> x0, matrix products: 24.9 us -> none  [the longest x10 22.7 us: multiply(): return jnp.dot(first, second, preferred_element_type=jnp.float32)]
    ppermute x0 -> x4, starting transfers between devices: none -> 13.6 us  [the longest x1 4.51 us: local(): right_lent = lax.ppermute(right_state[1], 'fsdp', swap)]
    pallas_call x0 -> x1, Pallas kernels: none -> 6.52 us  [work_on_block(): pl.pallas_call(block_kernel, out_shape=(square, square, square), in_specs...]
    another operation x4 -> x0, loops' own time: 6.04 us -> none  [the longest x2 6 us: local(): lax.cond(owned[slot_number], precondition, blank_update, left_new[slot_nu...]
    cond x8 -> x0, local copies, waits for them, and re-layouts: 4.28 us -> none  [the longest x2 2.59 us: local(): lax.cond(owned[slot_number], precondition, blank_update, left_new[slot_nu...]
    broadcast_in_dim x1 -> x0, other arithmetic: 4.24 us -> none  [local(): updates[None]]
  transfers between devices with their start and end apart: 4 -> 8, of which waited for: 4 -> 6; matrix products, arithmetic and copies ran while one was open for 3% -> 9% of each run, Pallas kernels for 0% -> 0%
where the time goes in v1:
time: 144 us; the launch traced here: 143 us
  starting transfers between devices  59.4 us (41%)
  waiting for transfers between devices  53.4 us (37%)
  local copies, waits for them, and re-layouts  11.6 us (8%)
  other arithmetic  9.63 us (7%)
  Pallas kernels  6.52 us (5%)
  between operations  2.68 us (2%)
    all_to_all x1, starting transfers between devices, local(): lax.all_to_all(pick(arrived, source_entry), 'fsdp', split_axis=0, concat_...  14.1 us
    ppermute x1, waiting for transfers between devices, local(): left_lent = lax.ppermute(left_state[1], 'fsdp', swap)  13.5 us
    all_to_all x1, starting transfers between devices, local(): lax.all_to_all(update_block.reshape(fsdp_count, shard_rows, block_width),...  13 us
    ppermute x1, waiting for transfers between devices, local(): left_back = lax.ppermute(left_done, 'fsdp', swap)  10.9 us
    all_to_all x1, starting transfers between devices, local(): lax.all_to_all(pick(grads, my_picked), 'rep', split_axis=0, concat_axis=0...  10.3 us
    ppermute x1, waiting for transfers between devices, local(): right_lent = lax.ppermute(right_state[1], 'fsdp', swap)  8.85 us
    all_to_all x1, waiting for transfers between devices, local(): lax.all_to_all(pick(grads, my_picked), 'rep', split_axis=0, concat_axis=0...  8.6 us
    all_to_all x1, starting transfers between devices, local(): lax.all_to_all(pick(returned_rows, worker), 'rep', split_axis=0, concat_a...  8.45 us
  transfers between devices with their start and end apart: 8, of which 6 were waited for; matrix products, arithmetic and copies ran while one was open for 9% of the time, Pallas kernels for 0%

profile of v1, /device:TPU:1, one launch (start us, length us, event | category | flops | bytes accessed | tf_op | source)
XLA Modules:
  0.0 143.2 jit_solution(14426733100002633959)
XLA Ops:
  1.8 1.4 gather_fusion
  3.2 10.3 %all-to-all-start = ((bf16[64,8,512]{2,1,0:T(8,128)(2,1)}), bf16[64,8,512]{2,1,0:T(8,128)(2,1)S(1)}, u32[]{:S(2)}, u32[]{:S(2)}) async-start(bf16[64,8,512]{2,1,0:T(8,128)(2,1)} %gather_fusion), calls=%async_computation | async-start | bytes 1048576 | tf_op jit(solution)/shard_map/all_to_all | solution.py:136
  14.4 8.6 %all-to-all-done = bf16[64,8,512]{2,1,0:T(8,128)(2,1)S(1)} async-done(((bf16[64,8,512]{2,1,0:T(8,128)(2,1)}), bf16[64,8,512]{2,1,0:T(8,128)(2,1)S(1)}, u32[]{:S(2)}, u32[]{:S(2)}) %all-to-all-start) | async-done | bytes 524320 | tf_op jit(solution)/shard_map/all_to_all | solution.py:136
  23.0 1.4 gather_fusion.1
  24.4 14.1 %all-to-all-start.1 = ((bf16[64,8,512]{2,1,0:T(8,128)(2,1)}), bf16[64,8,512]{2,1,0:T(8,128)(2,1)S(1)}, u32[]{:S(2)}, u32[]{:S(2)}) async-start(bf16[64,8,512]{2,1,0:T(8,128)(2,1)} %gather_fusion.1), calls=%async_computation.1 | async-start | bytes 1048576 | tf_op jit(solution)/shard_map/all_to_all | solution.py:153
  39.3 4.5 %collective-permute-start.1 = (bf16[512,512]{1,0:T(8,128)(2,1)}, bf16[512,512]{1,0:T(8,128)(2,1)}, u32[]{:S(2)}, u32[]{:S(2)}) collective-permute-start(bf16[512,512]{1,0:T(8,128)(2,1)} %slice_bitcast_fusion), channel_id=1, source_target_pairs={{0,256},{8,264},{16,272},{24,280},{32,288},{40,296},{48,304},{56,3... | collective-permute-start | bytes 1572872 | tf_op jit(solution)/shard_map/ppermute | solution.py:124
  43.9 0.8 slice_bitcast_fusion.1
  44.7 2.3 %collective-permute-start = (bf16[512,512]{1,0:T(8,128)(2,1)}, bf16[512,512]{1,0:T(8,128)(2,1)}, u32[]{:S(2)}, u32[]{:S(2)}) collective-permute-start(bf16[512,512]{1,0:T(8,128)(2,1)} %slice_bitcast_fusion.1), channel_id=1, source_target_pairs={{0,256},{8,264},{16,272},{24,280},{32,288},{40,296},{48,304},{56,3... | collective-permute-start | bytes 1572872 | tf_op jit(solution)/shard_map/ppermute | solution.py:123
  49.5 8.8 %collective-permute-done.1.right_lent = bf16[512,512]{1,0:T(8,128)(2,1)} collective-permute-done((bf16[512,512]{1,0:T(8,128)(2,1)}, bf16[512,512]{1,0:T(8,128)(2,1)}, u32[]{:S(2)}, u32[]{:S(2)}) %collective-permute-start.1) | collective-permute-done | bytes 524320 | tf_op jit(solution)/shard_map/ppermute | solution.py:124
  58.4 13.5 %collective-permute-done.left_lent = bf16[512,512]{1,0:T(8,128)(2,1)} collective-permute-done((bf16[512,512]{1,0:T(8,128)(2,1)}, bf16[512,512]{1,0:T(8,128)(2,1)}, u32[]{:S(2)}, u32[]{:S(2)}) %collective-permute-start) | collective-permute-done | bytes 524320 | tf_op jit(solution)/shard_map/ppermute | solution.py:123
  71.9 6.5 %block_step.1 = (bf16[512,512]{1,0:T(8,128)(2,1)S(1)}, bf16[512,512]{1,0:T(8,128)(2,1)S(1)}, bf16[512,512]{1,0:T(8,128)(2,1)S(1)}) custom-call(s32[2]{0:T(128)S(1)} %add_convert_fusion.choice, bf16[512,512]{1,0:T(8,128)(2,1)S(1)} %bitcast.60, bf16[2,512,512]{2,1,0:T(8,128)(2,1)S(1)} %copy-done.1, bf16[2,512,512]{2,1,0:T(8,128)(2,1)S(1)} %copy-done.2, ...), custom_call_target="tpu_custom_call" | custom-call | flops 3221225472 | bytes 3145728 | tf_op jit(solution)/shard_map/block_step/pallas_call | solution.py:85
  80.8 13.0 %all-to-all-start.2 = ((bf16[64,8,512]{2,1,0:T(8,128)(2,1)}), bf16[64,8,512]{2,1,0:T(8,128)(2,1)}, u32[]{:S(2)}, u32[]{:S(2)}) async-start(bf16[64,8,512]{2,1,0:T(8,128)(2,1)} %bitcast.61), calls=%async_computation.2 | async-start | bytes 1048576 | tf_op jit(solution)/shard_map/all_to_all | solution.py:166
  93.9 4.5 %collective-permute-start.2 = (bf16[512,512]{1,0:T(8,128)(2,1)}, bf16[512,512]{1,0:T(8,128)(2,1)}, u32[]{:S(2)}, u32[]{:S(2)}) collective-permute-start(bf16[512,512]{1,0:T(8,128)(2,1)} %copy-done.6), channel_id=1, source_target_pairs={{0,256},{8,264},{16,272},{24,280},{32,288},{40,296},{48,304},{56,3... | collective-permute-start | bytes 1572872 | tf_op jit(solution)/shard_map/ppermute | solution.py:170
  98.5 2.3 %collective-permute-start.3 = (bf16[512,512]{1,0:T(8,128)(2,1)S(1)}, bf16[512,512]{1,0:T(8,128)(2,1)}, u32[]{:S(2)}, u32[]{:S(2)}) collective-permute-start(bf16[512,512]{1,0:T(8,128)(2,1)S(1)} %copy-done.5), channel_id=1, source_target_pairs={{0,256},{8,264},{16,272},{24,280},{32,288},{40,296},{48,304},{56,3... | collective-permute-start | bytes 1572872 | tf_op jit(solution)/shard_map/ppermute | solution.py:171
  100.8 10.9 %collective-permute-done.2 = bf16[512,512]{1,0:T(8,128)(2,1)} collective-permute-done((bf16[512,512]{1,0:T(8,128)(2,1)}, bf16[512,512]{1,0:T(8,128)(2,1)}, u32[]{:S(2)}, u32[]{:S(2)}) %collective-permute-start.2) | collective-permute-done | bytes 524320 | tf_op jit(solution)/shard_map/ppermute | solution.py:170
  111.7 3.3 %fusion.1 = (bf16[1,512,512]{2,1,0:T(8,128)(2,1)}, bf16[1,512,512]{2,1,0:T(8,128)(2,1)}) fusion(bf16[512,512]{1,0:T(8,128)(2,1)} %copy-done.6, bf16[2,512,512]{2,1,0:T(8,128)(2,1)S(1)} %copy-done.1, pred[]{:T(512)} %get-tuple-element.10, bf16[512,512]{1,0:T(8,128)(2,1)} %collective-permute-done.2, pred[]{:T(512)} %get-tuple-element.9), kind=kLoop, calls=%fused_computation.9 | loop fusion | flops 786432 | bytes 3145730 | tf_op jit(solution)/shard_map/stack | solution.py:180
  115.0 6.5 %all-to-all-done.2 = bf16[64,8,512]{2,1,0:T(8,128)(2,1)} async-done(((bf16[64,8,512]{2,1,0:T(8,128)(2,1)}), bf16[64,8,512]{2,1,0:T(8,128)(2,1)}, u32[]{:S(2)}, u32[]{:S(2)}) %all-to-all-start.2) | async-done | bytes 524320 | tf_op jit(solution)/shard_map/all_to_all | solution.py:166
  121.5 2.4 %gather_fusion.2 = bf16[64,8,512]{2,1,0:T(8,128)(2,1)} fusion(bf16[64,8,512]{2,1,0:T(8,128)(2,1)} %all-to-all-done.2, s32[1024]{0:T(1024)S(1)} %pad_clamp_fusion.1), kind=kCustom, calls=%fused_computation.2 | custom fusion | bytes 1048832 | tf_op jit(solution)/shard_map/gather | solution.py:108
  123.9 8.5 %all-to-all-start.3 = ((bf16[64,8,512]{2,1,0:T(8,128)(2,1)}), bf16[64,8,512]{2,1,0:T(8,128)(2,1)S(1)}, u32[]{:S(2)}, u32[]{:S(2)}) async-start(bf16[64,8,512]{2,1,0:T(8,128)(2,1)} %gather_fusion.2), calls=%async_computation.3 | async-start | bytes 1048576 | tf_op jit(solution)/shard_map/all_to_all | solution.py:172
  132.4 2.1 %pad_maximum_fusion = bf16[2,512,512]{2,1,0:T(8,128)(2,1)} fusion(bf16[1,512,512]{2,1,0:T(8,128)(2,1)} %get-tuple-element.16, bf16[1,512,512]{2,1,0:T(8,128)(2,1)S(1)} %copy-done.7), kind=kLoop, calls=%fused_computation.4 | loop fusion | flops 524288 | bytes 2097152 | tf_op jit(solution)/shard_map/stack | solution.py:180
  134.5 1.3 fusion
  135.8 1.1 pad_maximum_fusion.1
  136.8 5.0 %all-to-all-done.3 = bf16[64,8,512]{2,1,0:T(8,128)(2,1)S(1)} async-done(((bf16[64,8,512]{2,1,0:T(8,128)(2,1)}), bf16[64,8,512]{2,1,0:T(8,128)(2,1)S(1)}, u32[]{:S(2)}, u32[]{:S(2)}) %all-to-all-start.3) | async-done | bytes 524320 | tf_op jit(solution)/shard_map/all_to_all | solution.py:172
  141.9 1.4 gather_fusion.3
  (46 shorter events, 6.1 us)
Async XLA Ops:
  0.6 1.2 copy-start
  0.7 0.7 copy-start.8
  3.2 19.8 %all-to-all-start = ((bf16[64,8,512]{2,1,0:T(8,128)(2,1)}), bf16[64,8,512]{2,1,0:T(8,128)(2,1)S(1)}, u32[]{:S(2)}, u32[]{:S(2)}) async-start(bf16[64,8,512]{2,1,0:T(8,128)(2,1)} %gather_fusion), calls=%async_computation | async-start | bytes 1048576 | tf_op jit(solution)/shard_map/all_to_all | solution.py:136
  14.4 24.1 %copy-start.2 = (bf16[2,512,512]{2,1,0:T(8,128)(2,1)S(1)}, bf16[2,512,512]{2,1,0:T(8,128)(2,1)}, u32[]{:S(2)}) copy-start(bf16[2,512,512]{2,1,0:T(8,128)(2,1)} %right_own.1) | copy-start | bytes 3145732
  24.4 19.5 %copy-start.1 = (bf16[2,512,512]{2,1,0:T(8,128)(2,1)S(1)}, bf16[2,512,512]{2,1,0:T(8,128)(2,1)}, u32[]{:S(2)}) copy-start(bf16[2,512,512]{2,1,0:T(8,128)(2,1)} %left_own.1) | copy-start | bytes 3145732
  24.4 47.5 %all-to-all-start.1 = ((bf16[64,8,512]{2,1,0:T(8,128)(2,1)}), bf16[64,8,512]{2,1,0:T(8,128)(2,1)S(1)}, u32[]{:S(2)}, u32[]{:S(2)}) async-start(bf16[64,8,512]{2,1,0:T(8,128)(2,1)} %gather_fusion.1), calls=%async_computation.1 | async-start | bytes 1048576 | tf_op jit(solution)/shard_map/all_to_all | solution.py:153
  39.3 19.0 %collective-permute-start.1 = (bf16[512,512]{1,0:T(8,128)(2,1)}, bf16[512,512]{1,0:T(8,128)(2,1)}, u32[]{:S(2)}, u32[]{:S(2)}) collective-permute-start(bf16[512,512]{1,0:T(8,128)(2,1)} %slice_bitcast_fusion), channel_id=1, source_target_pairs={{0,256},{8,264},{16,272},{24,280},{32,288},{40,296},{48,304},{56,3... | collective-permute-start | bytes 1572872 | tf_op jit(solution)/shard_map/ppermute | solution.py:124
  44.7 27.2 %collective-permute-start = (bf16[512,512]{1,0:T(8,128)(2,1)}, bf16[512,512]{1,0:T(8,128)(2,1)}, u32[]{:S(2)}, u32[]{:S(2)}) collective-permute-start(bf16[512,512]{1,0:T(8,128)(2,1)} %slice_bitcast_fusion.1), channel_id=1, source_target_pairs={{0,256},{8,264},{16,272},{24,280},{32,288},{40,296},{48,304},{56,3... | collective-permute-start | bytes 1572872 | tf_op jit(solution)/shard_map/ppermute | solution.py:123
  78.4 0.8 copy-start.3
  79.2 0.8 copy-start.4
  80.0 0.8 copy-start.6
  80.8 17.6 %copy-start.5 = (bf16[512,512]{1,0:T(8,128)(2,1)S(1)}, bf16[512,512]{1,0:T(8,128)(2,1)}, u32[]{:S(2)}) copy-start(bf16[512,512]{1,0:T(8,128)(2,1)} %copy-done.4) | copy-start | bytes 1572868
  80.8 40.7 %all-to-all-start.2 = ((bf16[64,8,512]{2,1,0:T(8,128)(2,1)}), bf16[64,8,512]{2,1,0:T(8,128)(2,1)}, u32[]{:S(2)}, u32[]{:S(2)}) async-start(bf16[64,8,512]{2,1,0:T(8,128)(2,1)} %bitcast.61), calls=%async_computation.2 | async-start | bytes 1048576 | tf_op jit(solution)/shard_map/all_to_all | solution.py:166
  93.9 17.8 %collective-permute-start.2 = (bf16[512,512]{1,0:T(8,128)(2,1)}, bf16[512,512]{1,0:T(8,128)(2,1)}, u32[]{:S(2)}, u32[]{:S(2)}) collective-permute-start(bf16[512,512]{1,0:T(8,128)(2,1)} %copy-done.6), channel_id=1, source_target_pairs={{0,256},{8,264},{16,272},{24,280},{32,288},{40,296},{48,304},{56,3... | collective-permute-start | bytes 1572872 | tf_op jit(solution)/shard_map/ppermute | solution.py:170
  98.5 36.0 %collective-permute-start.3 = (bf16[512,512]{1,0:T(8,128)(2,1)S(1)}, bf16[512,512]{1,0:T(8,128)(2,1)}, u32[]{:S(2)}, u32[]{:S(2)}) collective-permute-start(bf16[512,512]{1,0:T(8,128)(2,1)S(1)} %copy-done.5), channel_id=1, source_target_pairs={{0,256},{8,264},{16,272},{24,280},{32,288},{40,296},{48,304},{56,3... | collective-permute-start | bytes 1572872 | tf_op jit(solution)/shard_map/ppermute | solution.py:171
  123.9 8.5 %copy-start.7 = (bf16[1,512,512]{2,1,0:T(8,128)(2,1)S(1)}, bf16[1,512,512]{2,1,0:T(8,128)(2,1)}, u32[]{:S(2)}) copy-start(bf16[1,512,512]{2,1,0:T(8,128)(2,1)} %get-tuple-element.15) | copy-start | bytes 1572868
  123.9 17.9 %all-to-all-start.3 = ((bf16[64,8,512]{2,1,0:T(8,128)(2,1)}), bf16[64,8,512]{2,1,0:T(8,128)(2,1)S(1)}, u32[]{:S(2)}, u32[]{:S(2)}) async-start(bf16[64,8,512]{2,1,0:T(8,128)(2,1)} %gather_fusion.2), calls=%async_computation.3 | async-start | bytes 1048576 | tf_op jit(solution)/shard_map/all_to_all | solution.py:172

commit v2 on v1

v2 whole, which is shorter than its diff:
```python
import jax
import jax.numpy as jnp
from jax import lax
from jax.experimental import pallas as pl
from jax.experimental.pallas import tpu as pltpu
from jax.sharding import PartitionSpec as P

ITERS = 2
DECAY_RATE = 0.95
VMEM_LIMIT = 32 * 1024 * 1024


def multiply(first, second):
    return jnp.dot(first, second, preferred_element_type=jnp.float32)


def inverse_root(stored):
    factor = stored.astype(jnp.float32)
    scaling = 2.5 / jnp.sqrt(jnp.sum(factor * factor))
    current = scaling * factor
    width = factor.shape[0]
    rows = lax.broadcasted_iota(jnp.int32, (width, width), 0)
    columns = lax.broadcasted_iota(jnp.int32, (width, width), 1)
    five = jnp.where(rows == columns, 5.0, 0.0)
    result = None
    for iteration in range(ITERS):
        tangent = ((five - current) * 0.25).astype(jnp.bfloat16)
        if iteration == 0:
            result = tangent
        else:
            result = multiply(result, tangent).astype(jnp.bfloat16)
        if iteration + 1 < ITERS:
            square = multiply(tangent, tangent).astype(jnp.bfloat16)
            fourth = multiply(square, square).astype(jnp.bfloat16)
            current = multiply(fourth, current.astype(jnp.bfloat16))
    return result


def new_factors(gradient, left_old, right_old):
    left_gram = lax.dot_general(
        gradient, gradient, (((1,), (1,)), ((), ())), preferred_element_type=jnp.float32
    )
    left_factor = (
        DECAY_RATE * left_old.astype(jnp.float32) + (1.0 - DECAY_RATE) * left_gram
    ).astype(jnp.bfloat16)
    right_gram = lax.dot_general(
        gradient, gradient, (((0,), (0,)), ((), ())), preferred_element_type=jnp.float32
    )
    right_factor = (
        DECAY_RATE * right_old.astype(jnp.float32) + (1.0 - DECAY_RATE) * right_gram
    ).astype(jnp.bfloat16)
    return left_factor, right_factor


def block_kernel(
    choice, gradient_ref, left_own, right_own, lent_early, lent_late,
    update_out, left_out, right_out, gradient_out,
    left_old, right_old, left_new, right_new, update, old_sems, out_sems, update_sems,
):
    lent, slot = choice[0], choice[1]
    width = left_old.shape[0]
    early = lent_early.shape[0]

    @pl.when(lent == 1)
    def _():
        pltpu.make_async_copy(lent_early, left_old.at[:early], old_sems.at[0]).start()
        pltpu.make_async_copy(
            lent_late.at[: width - early], left_old.at[early:], old_sems.at[1]
        ).start()
        pltpu.make_async_copy(
            lent_late.at[width - early :], right_old, old_sems.at[2]
        ).start()

    @pl.when(lent == 0)
    def _():
        pltpu.make_async_copy(
            left_own.at[slot, :early], left_old.at[:early], old_sems.at[0]
        ).start()
        pltpu.make_async_copy(
            left_own.at[slot, early:], left_old.at[early:], old_sems.at[1]
        ).start()
        pltpu.make_async_copy(right_own.at[slot], right_old, old_sems.at[2]).start()

    keep_gradient = pltpu.make_async_copy(gradient_ref, gradient_out, out_sems.at[2])
    keep_gradient.start()
    pltpu.make_async_copy(lent_early, left_old.at[:early], old_sems.at[0]).wait()
    pltpu.make_async_copy(
        lent_late.at[: width - early], left_old.at[early:], old_sems.at[1]
    ).wait()
    pltpu.make_async_copy(lent_late.at[width - early :], right_old, old_sems.at[2]).wait()
    gradient = gradient_ref[...]
    left_factor, right_factor = new_factors(gradient, left_old[...], right_old[...])
    left_new[...] = left_factor
    right_new[...] = right_factor
    keep_left = pltpu.make_async_copy(left_new, left_out, out_sems.at[0])
    keep_right = pltpu.make_async_copy(right_new, right_out, out_sems.at[1])
    keep_left.start()
    keep_right.start()
    left_root = inverse_root(left_factor)
    right_root = inverse_root(right_factor)
    half_product = multiply(left_root, gradient).astype(jnp.bfloat16)
    raw_update = multiply(half_product, right_root)
    wide = gradient.astype(jnp.float32)
    grad_norm = jnp.sqrt(jnp.sum(wide * wide))
    raw_norm = jnp.sqrt(jnp.sum(raw_update * raw_update))
    scale = grad_norm / (raw_norm + 1e-06)
    sends = []
    part = width // update_sems.shape[0]
    for number in range(update_sems.shape[0]):
        rows = slice(number * part, (number + 1) * part)
        update[rows, :] = (raw_update[rows, :] * scale).astype(jnp.bfloat16)
        send = pltpu.make_async_copy(
            update.at[rows], update_out.at[rows], update_sems.at[number]
        )
        send.start()
        sends.append(send)
    for send in [keep_gradient, keep_left, keep_right] + sends:
        send.wait()


def work_on_block(choice, gradient, left_state, right_state, lent_early, lent_late):
    width = gradient.shape[0]
    square = pltpu.HBM((width, width), jnp.bfloat16)
    return pl.pallas_call(
        block_kernel,
        out_shape=(square,) * 4,
        in_specs=[
            pl.BlockSpec(memory_space=pltpu.SMEM),
            pl.BlockSpec(memory_space=pltpu.VMEM),
        ]
        + [pl.BlockSpec(memory_space=pl.ANY)] * 4,
        out_specs=[pl.BlockSpec(memory_space=pltpu.HBM)] * 4,
        scratch_shapes=[pltpu.VMEM((width, width), jnp.bfloat16)] * 5
        + [pltpu.SemaphoreType.DMA((3,)), pltpu.SemaphoreType.DMA((3,)), pltpu.SemaphoreType.DMA((4,))],
        compiler_params=pltpu.CompilerParams(vmem_limit_bytes=VMEM_LIMIT),
        cost_estimate=pl.CostEstimate(
            flops=24 * width**3, bytes_accessed=12 * width**2, transcendentals=0
        ),
        name="block_step",
    )(choice, gradient, left_state, right_state, lent_early, lent_late)


def settle_kernel(
    choice, gradient_back, left_own, right_own, left_done, right_done, left_out, right_out,
    gradient, left, right, sems,
):
    has_first, has_second = choice[2] == 1, choice[3] == 1
    has_both = has_first & has_second

    @pl.when(has_first)
    def _():
        pltpu.make_async_copy(left_done, left_out.at[0], sems.at[0]).start()
        pltpu.make_async_copy(right_done, right_out.at[0], sems.at[1]).start()

    @pl.when(~has_first)
    def _():
        pltpu.make_async_copy(left_own.at[0], left_out.at[0], sems.at[0]).start()
        pltpu.make_async_copy(right_own.at[0], right_out.at[0], sems.at[1]).start()

    @pl.when(has_second & ~has_first)
    def _():
        pltpu.make_async_copy(left_done, left_out.at[1], sems.at[2]).start()
        pltpu.make_async_copy(right_done, right_out.at[1], sems.at[3]).start()

    @pl.when(~has_second)
    def _():
        pltpu.make_async_copy(left_own.at[1], left_out.at[1], sems.at[2]).start()
        pltpu.make_async_copy(right_own.at[1], right_out.at[1], sems.at[3]).start()

    @pl.when(has_both)
    def _():
        loads = [
            pltpu.make_async_copy(left_own.at[1], left, sems.at[2]),
            pltpu.make_async_copy(right_own.at[1], right, sems.at[3]),
            pltpu.make_async_copy(gradient_back, gradient, sems.at[4]),
        ]
        for load in loads:
            load.start()
        for load in loads:
            load.wait()
        left_factor, right_factor = new_factors(gradient[...], left[...], right[...])
        left[...] = left_factor
        right[...] = right_factor
        pltpu.make_async_copy(left, left_out.at[1], sems.at[2]).start()
        pltpu.make_async_copy(right, right_out.at[1], sems.at[3]).start()

    for number, (source, target) in enumerate(
        [(left_done, left_out.at[0]), (right_done, right_out.at[0])]
        + [(left_done, left_out.at[1]), (right_done, right_out.at[1])]
    ):
        pltpu.make_async_copy(source, target, sems.at[number]).wait()


def settle(choice, gradient_back, left_state, right_state, left_done, right_done):
    slots, width, _ = left_state.shape
    both = pltpu.HBM(left_state.shape, jnp.bfloat16)
    return pl.pallas_call(
        settle_kernel,
        out_shape=(both, both),
        in_specs=[pl.BlockSpec(memory_space=pltpu.SMEM)]
        + [pl.BlockSpec(memory_space=pl.ANY)] * 5,
        out_specs=[pl.BlockSpec(memory_space=pltpu.HBM)] * 2,
        scratch_shapes=[pltpu.VMEM((width, width), jnp.bfloat16)] * 3
        + [pltpu.SemaphoreType.DMA((5,))],
        compiler_params=pltpu.CompilerParams(vmem_limit_bytes=VMEM_LIMIT),
        cost_estimate=pl.CostEstimate(
            flops=4 * width**3, bytes_accessed=16 * width**2, transcendentals=0
        ),
        name="settle_slots",
    )(choice, gradient_back, left_state, right_state, left_done, right_done)


def reorder_kernel(order, source, *rest):
    result, sem = rest[-2:]

    def move(number, carry):
        pltpu.make_async_copy(source.at[order[number]], result.at[number], sem).start()
        return carry

    lax.fori_loop(0, result.shape[0], move, 0, unroll=8)
    pltpu.make_async_copy(source, result, sem).wait()


def reorder(array, order, *needed):
    return pl.pallas_call(
        reorder_kernel,
        out_shape=pltpu.HBM(array.shape, array.dtype),
        in_specs=[pl.BlockSpec(memory_space=pltpu.SMEM)]
        + [pl.BlockSpec(memory_space=pl.ANY)] * (1 + len(needed)),
        out_specs=pl.BlockSpec(memory_space=pltpu.HBM),
        scratch_shapes=[pltpu.SemaphoreType.DMA],
        compiler_params=pltpu.CompilerParams(vmem_limit_bytes=VMEM_LIMIT // 4),
        name="reorder",
    )(order, array, *needed)


def local(grads, left_state, right_state, block_owner):
    rep_count = lax.axis_size("rep")
    fsdp_count = lax.axis_size("fsdp")
    group_index = lax.axis_index("rep")
    place_index = lax.axis_index("fsdp")
    held_blocks, shard_rows, block_width = grads.shape
    column_share = held_blocks // rep_count
    slot_count = left_state.shape[0]
    half = fsdp_count // 2
    swap = [(place, place ^ half) for place in range(fsdp_count)]
    positions = jnp.arange(held_blocks, dtype=jnp.int32)

    early = block_width // 2
    lent_early = lax.ppermute(left_state[1, :early], "fsdp", swap)
    lent_late = lax.ppermute(
        jnp.concatenate([left_state[1, early:], right_state[1]]), "fsdp", swap
    )

    owner_table = block_owner.reshape(rep_count, held_blocks)
    owner_column = owner_table // slot_count % rep_count
    before = positions[None, :] < positions[:, None]

    my_column = lax.dynamic_index_in_dim(owner_column, group_index, 0, keepdims=False)
    alike = (my_column[:, None] == my_column[None, :]) & before
    my_order = my_column * column_share + jnp.sum(alike.astype(jnp.int32), axis=1)
    my_picked = jnp.sum(
        jnp.where(my_order[None, :] == positions[:, None], positions[None, :], 0), axis=1
    )
    arrived = lax.all_to_all(
        reorder(pltpu.with_memory_space_constraint(grads, pltpu.HBM), my_picked),
        "rep", split_axis=0, concat_axis=0, tiled=True,
    )

    mine = owner_column == group_index
    rank = jnp.sum((mine[:, None, :] & before[None]).astype(jnp.int32), axis=2)
    shares = jnp.arange(column_share, dtype=jnp.int32)
    taken = mine[:, None, :] & (rank[:, None, :] == shares[None, :, None])
    entry_owner = jnp.sum(jnp.where(taken, owner_table[:, None, :], 0), axis=2).reshape(-1)

    sibling = jnp.any(entry_owner[None, :] == entry_owner[:, None] - 1, axis=1)
    second = (entry_owner % slot_count == 1) & sibling
    owner_place = entry_owner // (slot_count * rep_count)
    worker = jnp.where(second, owner_place ^ half, owner_place)
    source_entry = jnp.sum(
        jnp.where(worker[None, :] == positions[:, None], positions[None, :], 0), axis=1
    )
    gradient = lax.all_to_all(
        reorder(arrived, source_entry, lent_early),
        "fsdp", split_axis=0, concat_axis=0, tiled=True,
    ).reshape(fsdp_count * shard_rows, block_width)

    first_slot = (place_index * rep_count + group_index) * slot_count
    owns_first = jnp.any(entry_owner == first_slot)
    owns_second = jnp.any(entry_owner == first_slot + 1)
    lent = ~(owns_first | owns_second)
    choice = jnp.stack([lent, ~owns_first, owns_first, owns_second]).astype(jnp.int32)
    update_block, left_done, right_done, gradient = work_on_block(
        choice, gradient, left_state, right_state, lent_early, lent_late
    )

    returned_rows = lax.all_to_all(
        update_block.reshape(fsdp_count, shard_rows, block_width),
        "fsdp", split_axis=0, concat_axis=0, tiled=True,
    )
    gradient_back = lax.ppermute(gradient, "fsdp", swap)
    left_new, right_new = settle(
        choice, gradient_back, left_state, right_state, left_done, right_done
    )
    at_home = lax.all_to_all(
        reorder(returned_rows, worker), "rep", split_axis=0, concat_axis=0, tiled=True
    )
    update = reorder(at_home, my_order)
    return (update, left_new, right_new)


def solution(mesh):
    return jax.shard_map(
        local,
        mesh=mesh,
        in_specs=(
            P("rep", "fsdp", None),
            P(("fsdp", "rep"), None, None),
            P(("fsdp", "rep"), None, None),
            P(),
        ),
        out_specs=(
            P("rep", "fsdp", None),
            P(("fsdp", "rep"), None, None),
            P(("fsdp", "rep"), None, None),
        ),
        check_vma=False,
    )
```

time: 144 us -> 154 us (1.069)
  Pallas kernels: 6.52 us -> 31.6 us
  local copies, waits for them, and re-layouts: 11.6 us -> 1.97 us
  other arithmetic: 9.63 us -> 4.06 us
  waiting for transfers between devices: 53.4 us -> 55.6 us
  starting transfers between devices: 59.4 us -> 57.5 us
    pallas_call x1 -> x6, Pallas kernels: 6.52 us -> 31.6 us  [the longest x4 21.7 us: reorder(): pl.pallas_call(reorder_kernel, out_shape=pltpu.HBM(array.shape, array.dty...]
    all_to_all x1, waiting for transfers between devices: 6.51 us -> 22.9 us  [local(): lax.all_to_all(update_block.reshape(fsdp_count, shard_rows, block_width),...]
    another operation x4 -> x0, other arithmetic: 7.73 us -> none  [settled(): return jnp.stack([first, jnp.where(owns_second, other, state[1])])]
    all_to_all x3, waiting for transfers between devices: 13.6 us -> 6.04 us  [the longest x1 4.79 us: local(): lax.all_to_all(reorder(returned_rows, worker), 'rep', split_axis=0, conca...]
    gather x4 -> x0, local copies, waits for them, and re-layouts: 6.59 us -> none  [pick(): return array.at[order].get(mode='promise_in_bounds', unique_indices=True)]
    ppermute x4 -> x3, waiting for transfers between devices: 33.2 us -> 26.7 us  [the longest x1 18.3 us: local(): lax.ppermute(jnp.concatenate([left_state[1, early:], right_state[1]]), 'f...]
    ppermute x4 -> x3, starting transfers between devices: 13.6 us -> 11.1 us  [the longest x1 4.66 us: local(): gradient_back = lax.ppermute(gradient, 'fsdp', swap)]
    unnamed x18 -> x8, local copies, waits for them, and re-layouts: 3.13 us -> 1.06 us
  transfers between devices with their start and end apart: 8 -> 7, of which waited for: 6 -> 5; matrix products, arithmetic and copies ran while one was open for 9% -> 3% of each run, Pallas kernels for 0% -> 3%
where the time goes in v2:
time: 154 us
  starting transfers between devices  57.5 us (37%)
  waiting for transfers between devices  55.6 us (36%)
  Pallas kernels  31.6 us (21%)
  other arithmetic  4.06 us (3%)
  between operations  2.78 us (2%)
  local copies, waits for them, and re-layouts  1.97 us (1%)
    all_to_all x1, waiting for transfers between devices, local(): lax.all_to_all(update_block.reshape(fsdp_count, shard_rows, block_width),...  22.9 us
    pallas_call x4, Pallas kernels, reorder(): pl.pallas_call(reorder_kernel, out_shape=pltpu.HBM(array.shape, array.dty...  21.7 us
    ppermute x1, waiting for transfers between devices, local(): lax.ppermute(jnp.concatenate([left_state[1, early:], right_state[1]]), 'f...  18.3 us
    all_to_all x1, starting transfers between devices, local(): lax.all_to_all(reorder(arrived, source_entry, lent_early), 'fsdp', split_...  14.1 us
    all_to_all x1, starting transfers between devices, local(): lax.all_to_all(update_block.reshape(fsdp_count, shard_rows, block_width),...  12.8 us
    all_to_all x1, starting transfers between devices, local(): lax.all_to_all(reorder(pltpu.with_memory_space_constraint(grads, pltpu.HB...  10.3 us
    all_to_all x1, starting transfers between devices, local(): lax.all_to_all(reorder(returned_rows, worker), 'rep', split_axis=0, conca...  9.19 us
    ppermute x1, waiting for transfers between devices, local(): lent_early = lax.ppermute(left_state[1, :early], 'fsdp', swap)  8.36 us
  transfers between devices with their start and end apart: 7, of which 5 were waited for; matrix products, arithmetic and copies ran while one was open for 3% of the time, Pallas kernels for 3%

profile of v2, /device:TPU:1, one launch (start us, length us, event | category | flops | bytes accessed | tf_op | source)
XLA Modules:
  0.0 153.5 jit_solution(306174238202003846)
XLA Ops:
  0.6 0.8 reshape.137
  1.7 17.6 %reorder.4 = bf16[64,8,512]{2,1,0:T(8,128)(2,1)} custom-call(s32[64]{0:T(128)S(1)} %select_reduce_fusion.order, bf16[64,8,512]{2,1,0:T(8,128)(2,1)} %source.1), custom_call_target="tpu_custom_call" | custom-call | tf_op jit(solution)/shard_map/reorder/pallas_call | solution.py:225
  19.3 10.3 %all-to-all-start = ((bf16[64,8,512]{2,1,0:T(8,128)(2,1)}), bf16[64,8,512]{2,1,0:T(8,128)(2,1)S(1)}, u32[]{:S(2)}, u32[]{:S(2)}) async-start(bf16[64,8,512]{2,1,0:T(8,128)(2,1)} %reorder.4), calls=%async_computation | async-start | bytes 1048576 | tf_op jit(solution)/shard_map/all_to_all | solution.py:265
  29.6 1.9 %collective-permute-start = (bf16[256,512]{1,0:T(8,128)(2,1)S(1)}, bf16[256,512]{1,0:T(8,128)(2,1)S(1)}, u32[]{:S(2)}, u32[]{:S(2)}) collective-permute-start(bf16[256,512]{1,0:T(8,128)(2,1)S(1)} %get-tuple-element.20), channel_id=1, source_target_pairs={{0,256},{8,264},{16,272},{24,280},{32,288},{40,296},{48,304},{56,3... | collective-permute-start | bytes 786440 | tf_op jit(solution)/shard_map/ppermute | solution.py:250
  31.6 0.2 convert_reduce_fusion
  32.4 8.4 %collective-permute-done.rest_0_.lent_early = bf16[256,512]{1,0:T(8,128)(2,1)S(1)} collective-permute-done((bf16[256,512]{1,0:T(8,128)(2,1)S(1)}, bf16[256,512]{1,0:T(8,128)(2,1)S(1)}, u32[]{:S(2)}, u32[]{:S(2)}) %collective-permute-start) | collective-permute-done | bytes 262176 | tf_op jit(solution)/shard_map/ppermute | solution.py:250
  40.8 1.4 reorder.5
  42.2 14.1 %all-to-all-start.1 = ((bf16[64,8,512]{2,1,0:T(8,128)(2,1)}), bf16[64,8,512]{2,1,0:T(8,128)(2,1)S(1)}, u32[]{:S(2)}, u32[]{:S(2)}) async-start(bf16[64,8,512]{2,1,0:T(8,128)(2,1)} %reorder.5), calls=%async_computation.1 | async-start | bytes 1048576 | tf_op jit(solution)/shard_map/all_to_all | solution.py:283
  56.4 0.9 pad_maximum_fusion
  57.3 4.5 %collective-permute-start.1 = (bf16[768,512]{1,0:T(8,128)(2,1)}, bf16[768,512]{1,0:T(8,128)(2,1)}, u32[]{:S(2)}, u32[]{:S(2)}) collective-permute-start(bf16[768,512]{1,0:T(8,128)(2,1)} %pad_maximum_fusion), channel_id=1, source_target_pairs={{0,256},{8,264},{16,272},{24,280},{32,288},{40,296},{48,304},{56,3... | collective-permute-start | bytes 2359304 | tf_op jit(solution)/shard_map/ppermute | solution.py:251
  61.9 0.7 compare_reduce_fusion.2
  64.5 1.4 add_convert_fusion.choice
  65.9 18.3 %collective-permute-done.1.lent_late = bf16[768,512]{1,0:T(8,128)(2,1)} collective-permute-done((bf16[768,512]{1,0:T(8,128)(2,1)}, bf16[768,512]{1,0:T(8,128)(2,1)}, u32[]{:S(2)}, u32[]{:S(2)}) %collective-permute-start.1) | collective-permute-done | bytes 786464 | tf_op jit(solution)/shard_map/ppermute | solution.py:251
  84.2 1.3 all-to-all-done.1
  85.4 6.2 %block_step.1 = (bf16[512,512]{1,0:T(8,128)(2,1)}, bf16[512,512]{1,0:T(8,128)(2,1)}, bf16[512,512]{1,0:T(8,128)(2,1)}, bf16[512,512]{1,0:T(8,128)(2,1)}) custom-call(s32[4]{0:T(128)S(1)} %add_convert_fusion.choice, bf16[512,512]{1,0:T(8,128)(2,1)S(1)} %bitcast.22, bf16[2,512,512]{2,1,0:T(8,128)(2,1)S(1)} %copy-done, bf16[2,512,512]{2,1,0:T(8,128)(2,1)S(1)} %copy-done.1, ...), custom_call_target="tpu_custom_call" | custom-call | flops 3221225472 | bytes 3145728 | tf_op jit(solution)/shard_map/block_step/pallas_call | solution.py:124
  91.7 12.8 %all-to-all-start.2 = ((bf16[64,8,512]{2,1,0:T(8,128)(2,1)}), bf16[64,8,512]{2,1,0:T(8,128)(2,1)S(1)}, u32[]{:S(2)}, u32[]{:S(2)}) async-start(bf16[64,8,512]{2,1,0:T(8,128)(2,1)} %bitcast.23), calls=%async_computation.2 | async-start | bytes 1048576 | tf_op jit(solution)/shard_map/all_to_all | solution.py:297
  104.5 4.7 %collective-permute-start.2 = (bf16[512,512]{1,0:T(8,128)(2,1)}, bf16[512,512]{1,0:T(8,128)(2,1)}, u32[]{:S(2)}, u32[]{:S(2)}) collective-permute-start(bf16[512,512]{1,0:T(8,128)(2,1)} %get-tuple-element.10), channel_id=1, source_target_pairs={{0,256},{8,264},{16,272},{24,280},{32,288},{40,296},{48,304},{56,3... | collective-permute-start | bytes 1572872 | tf_op jit(solution)/shard_map/ppermute | solution.py:301
  109.2 22.9 %all-to-all-done.2.source = bf16[64,8,512]{2,1,0:T(8,128)(2,1)S(1)} async-done(((bf16[64,8,512]{2,1,0:T(8,128)(2,1)}), bf16[64,8,512]{2,1,0:T(8,128)(2,1)S(1)}, u32[]{:S(2)}, u32[]{:S(2)}) %all-to-all-start.2) | async-done | bytes 524320 | tf_op jit(solution)/shard_map/all_to_all | solution.py:297
  132.1 1.4 reorder.6
  133.5 9.2 %all-to-all-start.3 = ((bf16[64,8,512]{2,1,0:T(8,128)(2,1)}), bf16[64,8,512]{2,1,0:T(8,128)(2,1)S(1)}, u32[]{:S(2)}, u32[]{:S(2)}) async-start(bf16[64,8,512]{2,1,0:T(8,128)(2,1)} %reorder.6), calls=%async_computation.3 | async-start | bytes 1048576 | tf_op jit(solution)/shard_map/all_to_all | solution.py:305
  142.7 1.0 copy-done.3
  143.7 3.6 %settle_slots.1 = (bf16[2,512,512]{2,1,0:T(8,128)(2,1)}, bf16[2,512,512]{2,1,0:T(8,128)(2,1)}) custom-call(s32[4]{0:T(128)S(1)} %add_convert_fusion.choice, bf16[512,512]{1,0:T(8,128)(2,1)} %collective-permute-done.2.gradient_back, bf16[2,512,512]{2,1,0:T(8,128)(2,1)S(1)} %copy-done, bf16[2,512,512]{2,1,0:T(8,128)(2,1)S(1)} %copy-done.1, ...), custom_call_target="tpu_custom_call" | custom-call | flops 536870912 | bytes 4194304 | tf_op jit(solution)/shard_map/settle_slots/pallas_call | solution.py:197
  147.3 4.8 %all-to-all-done.3.source = bf16[64,8,512]{2,1,0:T(8,128)(2,1)S(1)} async-done(((bf16[64,8,512]{2,1,0:T(8,128)(2,1)}), bf16[64,8,512]{2,1,0:T(8,128)(2,1)S(1)}, u32[]{:S(2)}, u32[]{:S(2)}) %all-to-all-start.3) | async-done | bytes 524320 | tf_op jit(solution)/shard_map/all_to_all | solution.py:305
  152.1 1.4 reorder.7
  (24 shorter events, 1.0 us)
Async XLA Ops:
  1.7 27.9 %copy-start = (bf16[2,512,512]{2,1,0:T(8,128)(2,1)S(1)}, bf16[2,512,512]{2,1,0:T(8,128)(2,1)}, u32[]{:S(2)}) copy-start(bf16[2,512,512]{2,1,0:T(8,128)(2,1)} %left_own.3) | copy-start | bytes 3145732
  19.3 21.5 %all-to-all-start = ((bf16[64,8,512]{2,1,0:T(8,128)(2,1)}), bf16[64,8,512]{2,1,0:T(8,128)(2,1)S(1)}, u32[]{:S(2)}, u32[]{:S(2)}) async-start(bf16[64,8,512]{2,1,0:T(8,128)(2,1)} %reorder.4), calls=%async_computation | async-start | bytes 1048576 | tf_op jit(solution)/shard_map/all_to_all | solution.py:265
  29.6 11.2 %collective-permute-start = (bf16[256,512]{1,0:T(8,128)(2,1)S(1)}, bf16[256,512]{1,0:T(8,128)(2,1)S(1)}, u32[]{:S(2)}, u32[]{:S(2)}) collective-permute-start(bf16[256,512]{1,0:T(8,128)(2,1)S(1)} %get-tuple-element.20), channel_id=1, source_target_pairs={{0,256},{8,264},{16,272},{24,280},{32,288},{40,296},{48,304},{56,3... | collective-permute-start | bytes 786440 | tf_op jit(solution)/shard_map/ppermute | solution.py:250
  32.4 23.9 %copy-start.1 = (bf16[2,512,512]{2,1,0:T(8,128)(2,1)S(1)}, bf16[2,512,512]{2,1,0:T(8,128)(2,1)}, u32[]{:S(2)}) copy-start(bf16[2,512,512]{2,1,0:T(8,128)(2,1)} %right_own.3) | copy-start | bytes 3145732
  42.2 43.2 %all-to-all-start.1 = ((bf16[64,8,512]{2,1,0:T(8,128)(2,1)}), bf16[64,8,512]{2,1,0:T(8,128)(2,1)S(1)}, u32[]{:S(2)}, u32[]{:S(2)}) async-start(bf16[64,8,512]{2,1,0:T(8,128)(2,1)} %reorder.5), calls=%async_computation.1 | async-start | bytes 1048576 | tf_op jit(solution)/shard_map/all_to_all | solution.py:283
  57.3 26.9 %collective-permute-start.1 = (bf16[768,512]{1,0:T(8,128)(2,1)}, bf16[768,512]{1,0:T(8,128)(2,1)}, u32[]{:S(2)}, u32[]{:S(2)}) collective-permute-start(bf16[768,512]{1,0:T(8,128)(2,1)} %pad_maximum_fusion), channel_id=1, source_target_pairs={{0,256},{8,264},{16,272},{24,280},{32,288},{40,296},{48,304},{56,3... | collective-permute-start | bytes 2359304 | tf_op jit(solution)/shard_map/ppermute | solution.py:251
  91.7 40.4 %all-to-all-start.2 = ((bf16[64,8,512]{2,1,0:T(8,128)(2,1)}), bf16[64,8,512]{2,1,0:T(8,128)(2,1)S(1)}, u32[]{:S(2)}, u32[]{:S(2)}) async-start(bf16[64,8,512]{2,1,0:T(8,128)(2,1)} %bitcast.23), calls=%async_computation.2 | async-start | bytes 1048576 | tf_op jit(solution)/shard_map/all_to_all | solution.py:297
  104.5 38.2 %copy-start.2 = (bf16[512,512]{1,0:T(8,128)(2,1)S(1)}, bf16[512,512]{1,0:T(8,128)(2,1)}, u32[]{:S(2)}) copy-start(bf16[512,512]{1,0:T(8,128)(2,1)} %get-tuple-element.11.left_done) | copy-start | bytes 1572868
  104.5 38.1 %collective-permute-start.2 = (bf16[512,512]{1,0:T(8,128)(2,1)}, bf16[512,512]{1,0:T(8,128)(2,1)}, u32[]{:S(2)}, u32[]{:S(2)}) collective-permute-start(bf16[512,512]{1,0:T(8,128)(2,1)} %get-tuple-element.10), channel_id=1, source_target_pairs={{0,256},{8,264},{16,272},{24,280},{32,288},{40,296},{48,304},{56,3... | collective-permute-start | bytes 1572872 | tf_op jit(solution)/shard_map/ppermute | solution.py:301
  133.5 18.7 %all-to-all-start.3 = ((bf16[64,8,512]{2,1,0:T(8,128)(2,1)}), bf16[64,8,512]{2,1,0:T(8,128)(2,1)S(1)}, u32[]{:S(2)}, u32[]{:S(2)}) async-start(bf16[64,8,512]{2,1,0:T(8,128)(2,1)} %reorder.6), calls=%async_computation.3 | async-start | bytes 1048576 | tf_op jit(solution)/shard_map/all_to_all | solution.py:305
  142.7 1.0 copy-start.3

commit v3 on v2

--- a/solution.py
+++ b/solution.py
@@ -8,6 +8,7 @@
 ITERS = 2
 DECAY_RATE = 0.95
 VMEM_LIMIT = 32 * 1024 * 1024
+EARLY_ROWS = 448
 
 
 def multiply(first, second):
@@ -36,20 +37,20 @@
     return result
 
 
-def new_factors(gradient, left_old, right_old):
-    left_gram = lax.dot_general(
+def grams(gradient):
+    left = lax.dot_general(
         gradient, gradient, (((1,), (1,)), ((), ())), preferred_element_type=jnp.float32
     )
-    left_factor = (
-        DECAY_RATE * left_old.astype(jnp.float32) + (1.0 - DECAY_RATE) * left_gram
+    right = lax.dot_general(
+        gradient, gradient, (((0,), (0,)), ((), ())), preferred_element_type=jnp.float32
+    )
+    return left, right
+
+
+def blend(old, gram):
+    return (
+        DECAY_RATE * old.astype(jnp.float32) + (1.0 - DECAY_RATE) * gram
     ).astype(jnp.bfloat16)
-    right_gram = lax.dot_general(
-        gradient, gradient, (((0,), (0,)), ((), ())), preferred_element_type=jnp.float32
-    )
-    right_factor = (
-        DECAY_RATE * right_old.astype(jnp.float32) + (1.0 - DECAY_RATE) * right_gram
-    ).astype(jnp.bfloat16)
-    return left_factor, right_factor
 
 
 def block_kernel(
@@ -89,7 +90,9 @@
     ).wait()
     pltpu.make_async_copy(lent_late.at[width - early :], right_old, old_sems.at[2]).wait()
     gradient = gradient_ref[...]
-    left_factor, right_factor = new_factors(gradient, left_old[...], right_old[...])
+    left_gram, right_gram = grams(gradient)
+    left_factor = blend(left_old[...], left_gram)
+    right_factor = blend(right_old[...], right_gram)
     left_new[...] = left_factor
     right_new[...] = right_factor
     keep_left = pltpu.make_async_copy(left_new, left_out, out_sems.at[0])
@@ -178,9 +181,9 @@
             load.start()
         for load in loads:
             load.wait()
-        left_factor, right_factor = new_factors(gradient[...], left[...], right[...])
-        left[...] = left_factor
-        right[...] = right_factor
+        left_gram, right_gram = grams(gradient[...])
+        left[...] = blend(left[...], left_gram)
+        right[...] = blend(right[...], right_gram)
         pltpu.make_async_copy(left, left_out.at[1], sems.at[2]).start()
         pltpu.make_async_copy(right, right_out.at[1], sems.at[3]).start()
 
@@ -234,6 +237,42 @@
     )(order, array, *needed)
 
 
+def late_loan_kernel(left_own, right_own, result, held, sems):
+    width = right_own.shape[1]
+    rest = held.shape[0] - width
+    loads = [
+        pltpu.make_async_copy(
+            left_own.at[1, width - rest :], held.at[:rest], sems.at[0]
+        ),
+        pltpu.make_async_copy(right_own.at[1], held.at[rest:], sems.at[1]),
+    ]
+    for load in loads:
+        load.start()
+    for load in loads:
+        load.wait()
+    store = pltpu.make_async_copy(held, result, sems.at[2])
+    store.start()
+    store.wait()
+
+
+def late_loan(left_state, right_state, early):
+    width = left_state.shape[1]
+    shape = (2 * width - early, width)
+    return pl.pallas_call(
+        late_loan_kernel,
+        out_shape=pltpu.HBM(shape, jnp.bfloat16),
+        in_specs=[pl.BlockSpec(memory_space=pl.ANY)] * 2,
+        out_specs=pl.BlockSpec(memory_space=pltpu.HBM),
+        scratch_shapes=[pltpu.VMEM(shape, jnp.bfloat16), pltpu.SemaphoreType.DMA((3,))],
+        compiler_params=pltpu.CompilerParams(vmem_limit_bytes=VMEM_LIMIT // 4),
+        name="late_loan",
+    )(left_state, right_state)
+
+
+def pick(array, order):
+    return array.at[order].get(mode="promise_in_bounds", unique_indices=True)
+
+
 def local(grads, left_state, right_state, block_owner):
     rep_count = lax.axis_size("rep")
     fsdp_count = lax.axis_size("fsdp")
@@ -246,11 +285,9 @@
     swap = [(place, place ^ half) for place in range(fsdp_count)]
     positions = jnp.arange(held_blocks, dtype=jnp.int32)
 
-    early = block_width // 2
+    early = EARLY_ROWS
     lent_early = lax.ppermute(left_state[1, :early], "fsdp", swap)
-    lent_late = lax.ppermute(
-        jnp.concatenate([left_state[1, early:], right_state[1]]), "fsdp", swap
-    )
+    lent_late = lax.ppermute(late_loan(left_state, right_state, early), "fsdp", swap)
 
     owner_table = block_owner.reshape(rep_count, held_blocks)
     owner_column = owner_table // slot_count % rep_count
@@ -263,7 +300,7 @@
         jnp.where(my_order[None, :] == positions[:, None], positions[None, :], 0), axis=1
     )
     arrived = lax.all_to_all(
-        reorder(pltpu.with_memory_space_constraint(grads, pltpu.HBM), my_picked),
+        pick(grads, my_picked),
         "rep", split_axis=0, concat_axis=0, tiled=True,
     )
 

time: 154 us -> 137 us (0.89)
  Pallas kernels: 31.6 us -> 14.6 us
  starting transfers between devices: 57.5 us -> 52.3 us
  local copies, waits for them, and re-layouts: 1.97 us -> 6.2 us
    pallas_call x4 -> x3, Pallas kernels: 21.7 us -> 4.15 us  [reorder(): pl.pallas_call(reorder_kernel, out_shape=pltpu.HBM(array.shape, array.dty...]
    all_to_all x1, waiting for transfers between devices: 0.01 us -> 8.6 us  [local(): lax.all_to_all(pick(grads, my_picked), 'rep', split_axis=0, concat_axis=0...]
    ppermute x1, waiting for transfers between devices: 8.36 us -> 0.01 us  [local(): lent_early = lax.ppermute(left_state[1, :early], 'fsdp', swap)]
    all_to_all x1, waiting for transfers between devices: 1.25 us -> 6.85 us  [local(): lax.all_to_all(reorder(arrived, source_entry, lent_early), 'fsdp', split_...]
    ppermute x1, waiting for transfers between devices: 18.3 us -> 12.9 us  [local(): lax.ppermute(late_loan(left_state, right_state, early), 'fsdp', swap)]
    all_to_all x1, starting transfers between devices: 12.8 us -> 8.09 us  [local(): lax.all_to_all(update_block.reshape(fsdp_count, shard_rows, block_width),...]
    all_to_all x1, starting transfers between devices: 10.3 us -> 6.54 us  [local(): lax.all_to_all(pick(grads, my_picked), 'rep', split_axis=0, concat_axis=0...]
    ppermute x1, starting transfers between devices: 1.92 us -> 5.64 us  [local(): lent_early = lax.ppermute(left_state[1, :early], 'fsdp', swap)]
where the time goes in v3:
time: 137 us; the launch traced here: 136 us
  waiting for transfers between devices  57.1 us (42%)
  starting transfers between devices  52.3 us (38%)
  Pallas kernels  14.6 us (11%)
  local copies, waits for them, and re-layouts  6.2 us (5%)
  other arithmetic  3 us (2%)
  between operations  2.73 us (2%)
    all_to_all x1, waiting for transfers between devices, local(): lax.all_to_all(update_block.reshape(fsdp_count, shard_rows, block_width),...  23.2 us
    all_to_all x1, starting transfers between devices, local(): lax.all_to_all(reorder(arrived, source_entry, lent_early), 'fsdp', split_...  15 us
    ppermute x1, waiting for transfers between devices, local(): lax.ppermute(late_loan(left_state, right_state, early), 'fsdp', swap)  12.9 us
    all_to_all x1, waiting for transfers between devices, local(): lax.all_to_all(pick(grads, my_picked), 'rep', split_axis=0, concat_axis=0...  8.6 us
    all_to_all x1, starting transfers between devices, local(): lax.all_to_all(update_block.reshape(fsdp_count, shard_rows, block_width),...  8.09 us
    all_to_all x1, starting transfers between devices, local(): lax.all_to_all(reorder(returned_rows, worker), 'rep', split_axis=0, conca...  7.94 us
    pallas_call x1, Pallas kernels, work_on_block(): pl.pallas_call(block_kernel, out_shape=(square,) * 4, in_specs=[pl.BlockS...  7.55 us
    all_to_all x1, waiting for transfers between devices, local(): lax.all_to_all(reorder(arrived, source_entry, lent_early), 'fsdp', split_...  6.85 us
  transfers between devices with their start and end apart: 7, of which 5 were waited for; matrix products, arithmetic and copies ran while one was open for 3% of the time, Pallas kernels for 3%

profile of v3, /device:TPU:1, one launch (start us, length us, event | category | flops | bytes accessed | tf_op | source)
XLA Modules:
  0.0 135.8 jit_solution(1346609231529699067)
XLA Ops:
  0.6 1.9 %slice_bitcast_fusion = bf16[448,512]{1,0:T(8,128)(2,1)} fusion(bf16[2,512,512]{2,1,0:T(8,128)(2,1)} %left_own.5), kind=kLoop, calls=%fused_computation.1 | loop fusion | bytes 917504 | tf_op jit(solution)/shard_map/squeeze | solution.py:289
  2.5 5.6 %collective-permute-start = (bf16[448,512]{1,0:T(8,128)(2,1)}, bf16[448,512]{1,0:T(8,128)(2,1)}, u32[]{:S(2)}, u32[]{:S(2)}) collective-permute-start(bf16[448,512]{1,0:T(8,128)(2,1)} %slice_bitcast_fusion), channel_id=1, source_target_pairs={{0,256},{8,264},{16,272},{24,280},{32,288},{40,296},{48,304},{56,3... | collective-permute-start | bytes 1376264 | tf_op jit(solution)/shard_map/ppermute | solution.py:289
  8.2 0.7 copy-done.5
  9.3 1.4 %gather_fusion = bf16[64,8,512]{2,1,0:T(8,128)(2,1)} fusion(bf16[64,8,512]{2,1,0:T(8,128)(2,1)S(1)} %copy-done, s32[1024]{0:T(1024)S(1)} %pad_clamp_fusion), kind=kCustom, calls=%fused_computation | custom fusion | bytes 1048832 | tf_op jit(solution)/shard_map/gather | solution.py:273
  10.7 6.5 %all-to-all-start = ((bf16[64,8,512]{2,1,0:T(8,128)(2,1)}), bf16[64,8,512]{2,1,0:T(8,128)(2,1)S(1)}, u32[]{:S(2)}, u32[]{:S(2)}) async-start(bf16[64,8,512]{2,1,0:T(8,128)(2,1)} %gather_fusion), calls=%async_computation | async-start | bytes 1048576 | tf_op jit(solution)/shard_map/all_to_all | solution.py:302
  18.1 8.6 %all-to-all-done.source = bf16[64,8,512]{2,1,0:T(8,128)(2,1)S(1)} async-done(((bf16[64,8,512]{2,1,0:T(8,128)(2,1)}), bf16[64,8,512]{2,1,0:T(8,128)(2,1)S(1)}, u32[]{:S(2)}, u32[]{:S(2)}) %all-to-all-start) | async-done | bytes 524320 | tf_op jit(solution)/shard_map/all_to_all | solution.py:302
  26.7 1.4 %reorder.3 = bf16[64,8,512]{2,1,0:T(8,128)(2,1)} custom-call(s32[64]{0:T(128)S(1)} %select_reduce_fusion.1.order, bf16[64,8,512]{2,1,0:T(8,128)(2,1)S(1)} %all-to-all-done.source, bf16[448,512]{1,0:T(8,128)(2,1)} %collective-permute-done.rest_0_.lent_early), custom_call_target="tpu_custom_call" | custom-call | tf_op jit(solution)/shard_map/reorder/pallas_call | solution.py:228
  28.1 15.0 %all-to-all-start.1 = ((bf16[64,8,512]{2,1,0:T(8,128)(2,1)}), bf16[64,8,512]{2,1,0:T(8,128)(2,1)S(1)}, u32[]{:S(2)}, u32[]{:S(2)}) async-start(bf16[64,8,512]{2,1,0:T(8,128)(2,1)} %reorder.3), calls=%async_computation.1 | async-start | bytes 1048576 | tf_op jit(solution)/shard_map/all_to_all | solution.py:320
  43.2 1.0 late_loan.1
  44.2 4.5 %collective-permute-start.1 = (bf16[576,512]{1,0:T(8,128)(2,1)}, bf16[576,512]{1,0:T(8,128)(2,1)}, u32[]{:S(2)}, u32[]{:S(2)}) collective-permute-start(bf16[576,512]{1,0:T(8,128)(2,1)} %late_loan.1), channel_id=1, source_target_pairs={{0,256},{8,264},{16,272},{24,280},{32,288},{40,296},{48,304},{56,3... | collective-permute-start | bytes 1769480 | tf_op jit(solution)/shard_map/ppermute | solution.py:290
  51.2 1.3 add_convert_fusion.choice
  52.5 12.9 %collective-permute-done.1.lent_late = bf16[576,512]{1,0:T(8,128)(2,1)} collective-permute-done((bf16[576,512]{1,0:T(8,128)(2,1)}, bf16[576,512]{1,0:T(8,128)(2,1)}, u32[]{:S(2)}, u32[]{:S(2)}) %collective-permute-start.1) | collective-permute-done | bytes 589856 | tf_op jit(solution)/shard_map/ppermute | solution.py:290
  65.3 6.8 %all-to-all-done.1 = bf16[64,8,512]{2,1,0:T(8,128)(2,1)S(1)} async-done(((bf16[64,8,512]{2,1,0:T(8,128)(2,1)}), bf16[64,8,512]{2,1,0:T(8,128)(2,1)S(1)}, u32[]{:S(2)}, u32[]{:S(2)}) %all-to-all-start.1) | async-done | bytes 524320 | tf_op jit(solution)/shard_map/all_to_all | solution.py:320
  72.2 7.6 %block_step.1 = (bf16[512,512]{1,0:T(8,128)(2,1)}, bf16[512,512]{1,0:T(8,128)(2,1)}, bf16[512,512]{1,0:T(8,128)(2,1)}, bf16[512,512]{1,0:T(8,128)(2,1)}) custom-call(s32[4]{0:T(128)S(1)} %add_convert_fusion.choice, bf16[512,512]{1,0:T(8,128)(2,1)S(1)} %bitcast.22, bf16[2,512,512]{2,1,0:T(8,128)(2,1)S(1)} %copy-done.1, bf16[2,512,512]{2,1,0:T(8,128)(2,1)S(1)} %copy-done.2, ...), custom_call_target="tpu_custom_call" | custom-call | flops 3221225472 | bytes 3145728 | tf_op jit(solution)/shard_map/block_step/pallas_call | solution.py:127
  79.8 8.1 %all-to-all-start.2 = ((bf16[64,8,512]{2,1,0:T(8,128)(2,1)}), bf16[64,8,512]{2,1,0:T(8,128)(2,1)S(1)}, u32[]{:S(2)}, u32[]{:S(2)}) async-start(bf16[64,8,512]{2,1,0:T(8,128)(2,1)} %bitcast.23), calls=%async_computation.2 | async-start | bytes 1048576 | tf_op jit(solution)/shard_map/all_to_all | solution.py:334
  87.8 4.5 %collective-permute-start.2 = (bf16[512,512]{1,0:T(8,128)(2,1)}, bf16[512,512]{1,0:T(8,128)(2,1)}, u32[]{:S(2)}, u32[]{:S(2)}) collective-permute-start(bf16[512,512]{1,0:T(8,128)(2,1)} %get-tuple-element.10), channel_id=1, source_target_pairs={{0,256},{8,264},{16,272},{24,280},{32,288},{40,296},{48,304},{56,3... | collective-permute-start | bytes 1572872 | tf_op jit(solution)/shard_map/ppermute | solution.py:338
  92.4 23.2 %all-to-all-done.2.source = bf16[64,8,512]{2,1,0:T(8,128)(2,1)S(1)} async-done(((bf16[64,8,512]{2,1,0:T(8,128)(2,1)}), bf16[64,8,512]{2,1,0:T(8,128)(2,1)S(1)}, u32[]{:S(2)}, u32[]{:S(2)}) %all-to-all-start.2) | async-done | bytes 524320 | tf_op jit(solution)/shard_map/all_to_all | solution.py:334
  115.6 1.4 %reorder.4 = bf16[64,8,512]{2,1,0:T(8,128)(2,1)} custom-call(s32[64]{0:T(128)S(1)} %and_select_fusion.1.order, bf16[64,8,512]{2,1,0:T(8,128)(2,1)S(1)} %all-to-all-done.2.source), custom_call_target="tpu_custom_call" | custom-call | tf_op jit(solution)/shard_map/reorder/pallas_call | solution.py:228
  117.0 7.9 %all-to-all-start.3 = ((bf16[64,8,512]{2,1,0:T(8,128)(2,1)}), bf16[64,8,512]{2,1,0:T(8,128)(2,1)S(1)}, u32[]{:S(2)}, u32[]{:S(2)}) async-start(bf16[64,8,512]{2,1,0:T(8,128)(2,1)} %reorder.4), calls=%async_computation.3 | async-start | bytes 1048576 | tf_op jit(solution)/shard_map/all_to_all | solution.py:342
  125.0 1.0 copy-done.3
  126.0 1.0 copy-done.4
  127.1 1.9 %settle_slots.1 = (bf16[2,512,512]{2,1,0:T(8,128)(2,1)}, bf16[2,512,512]{2,1,0:T(8,128)(2,1)}) custom-call(s32[4]{0:T(128)S(1)} %add_convert_fusion.choice, bf16[512,512]{1,0:T(8,128)(2,1)} %collective-permute-done.2.gradient_back, bf16[2,512,512]{2,1,0:T(8,128)(2,1)S(1)} %copy-done.1, bf16[2,512,512]{2,1,0:T(8,128)(2,1)S(1)} %copy-done.2, ...), custom_call_target="tpu_custom_call" | custom-call | flops 536870912 | bytes 4194304 | tf_op jit(solution)/shard_map/settle_slots/pallas_call | solution.py:200
  129.0 5.5 %all-to-all-done.3.source = bf16[64,8,512]{2,1,0:T(8,128)(2,1)S(1)} async-done(((bf16[64,8,512]{2,1,0:T(8,128)(2,1)}), bf16[64,8,512]{2,1,0:T(8,128)(2,1)S(1)}, u32[]{:S(2)}, u32[]{:S(2)}) %all-to-all-start.3) | async-done | bytes 524320 | tf_op jit(solution)/shard_map/all_to_all | solution.py:342
  134.5 1.4 %reorder.5 = bf16[64,8,512]{2,1,0:T(8,128)(2,1)} custom-call(s32[64]{0:T(128)S(1)} %multiply_add_fusion.order, bf16[64,8,512]{2,1,0:T(8,128)(2,1)S(1)} %all-to-all-done.3.source), custom_call_target="tpu_custom_call" | custom-call | tf_op jit(solution)/shard_map/reorder/pallas_call | solution.py:228
  (29 shorter events, 1.9 us)
Async XLA Ops:
  0.6 8.7 %copy-start = (bf16[64,8,512]{2,1,0:T(8,128)(2,1)S(1)}, bf16[64,8,512]{2,1,0:T(8,128)(2,1)}, u32[]{:S(2)}) copy-start(bf16[64,8,512]{2,1,0:T(8,128)(2,1)} %param.4) | copy-start | bytes 1572868
  2.5 15.6 %collective-permute-start = (bf16[448,512]{1,0:T(8,128)(2,1)}, bf16[448,512]{1,0:T(8,128)(2,1)}, u32[]{:S(2)}, u32[]{:S(2)}) collective-permute-start(bf16[448,512]{1,0:T(8,128)(2,1)} %slice_bitcast_fusion), channel_id=1, source_target_pairs={{0,256},{8,264},{16,272},{24,280},{32,288},{40,296},{48,304},{56,3... | collective-permute-start | bytes 1376264 | tf_op jit(solution)/shard_map/ppermute | solution.py:289
  8.2 0.7 copy-start.5
  10.7 16.0 %all-to-all-start = ((bf16[64,8,512]{2,1,0:T(8,128)(2,1)}), bf16[64,8,512]{2,1,0:T(8,128)(2,1)S(1)}, u32[]{:S(2)}, u32[]{:S(2)}) async-start(bf16[64,8,512]{2,1,0:T(8,128)(2,1)} %gather_fusion), calls=%async_computation | async-start | bytes 1048576 | tf_op jit(solution)/shard_map/all_to_all | solution.py:302
  18.1 25.1 %copy-start.1 = (bf16[2,512,512]{2,1,0:T(8,128)(2,1)S(1)}, bf16[2,512,512]{2,1,0:T(8,128)(2,1)}, u32[]{:S(2)}) copy-start(bf16[2,512,512]{2,1,0:T(8,128)(2,1)} %left_own.5) | copy-start | bytes 3145732
  18.1 25.1 %copy-start.2 = (bf16[2,512,512]{2,1,0:T(8,128)(2,1)S(1)}, bf16[2,512,512]{2,1,0:T(8,128)(2,1)}, u32[]{:S(2)}) copy-start(bf16[2,512,512]{2,1,0:T(8,128)(2,1)} %right_own.5) | copy-start | bytes 3145732
  28.1 44.1 %all-to-all-start.1 = ((bf16[64,8,512]{2,1,0:T(8,128)(2,1)}), bf16[64,8,512]{2,1,0:T(8,128)(2,1)S(1)}, u32[]{:S(2)}, u32[]{:S(2)}) async-start(bf16[64,8,512]{2,1,0:T(8,128)(2,1)} %reorder.3), calls=%async_computation.1 | async-start | bytes 1048576 | tf_op jit(solution)/shard_map/all_to_all | solution.py:320
  44.2 21.2 %collective-permute-start.1 = (bf16[576,512]{1,0:T(8,128)(2,1)}, bf16[576,512]{1,0:T(8,128)(2,1)}, u32[]{:S(2)}, u32[]{:S(2)}) collective-permute-start(bf16[576,512]{1,0:T(8,128)(2,1)} %late_loan.1), channel_id=1, source_target_pairs={{0,256},{8,264},{16,272},{24,280},{32,288},{40,296},{48,304},{56,3... | collective-permute-start | bytes 1769480 | tf_op jit(solution)/shard_map/ppermute | solution.py:290
  79.8 35.9 %all-to-all-start.2 = ((bf16[64,8,512]{2,1,0:T(8,128)(2,1)}), bf16[64,8,512]{2,1,0:T(8,128)(2,1)S(1)}, u32[]{:S(2)}, u32[]{:S(2)}) async-start(bf16[64,8,512]{2,1,0:T(8,128)(2,1)} %bitcast.23), calls=%async_computation.2 | async-start | bytes 1048576 | tf_op jit(solution)/shard_map/all_to_all | solution.py:334
  87.8 37.1 %collective-permute-start.2 = (bf16[512,512]{1,0:T(8,128)(2,1)}, bf16[512,512]{1,0:T(8,128)(2,1)}, u32[]{:S(2)}, u32[]{:S(2)}) collective-permute-start(bf16[512,512]{1,0:T(8,128)(2,1)} %get-tuple-element.10), channel_id=1, source_target_pairs={{0,256},{8,264},{16,272},{24,280},{32,288},{40,296},{48,304},{56,3... | collective-permute-start | bytes 1572872 | tf_op jit(solution)/shard_map/ppermute | solution.py:338
  117.0 17.4 %all-to-all-start.3 = ((bf16[64,8,512]{2,1,0:T(8,128)(2,1)}), bf16[64,8,512]{2,1,0:T(8,128)(2,1)S(1)}, u32[]{:S(2)}, u32[]{:S(2)}) async-start(bf16[64,8,512]{2,1,0:T(8,128)(2,1)} %reorder.4), calls=%async_computation.3 | async-start | bytes 1048576 | tf_op jit(solution)/shard_map/all_to_all | solution.py:342
  125.0 1.0 copy-start.3
  126.0 1.0 copy-start.4

commit v4 on v3

--- a/solution.py
+++ b/solution.py
@@ -1,3 +1,5 @@
+import functools
+
 import jax
 import jax.numpy as jnp
 from jax import lax
@@ -9,6 +11,13 @@
 DECAY_RATE = 0.95
 VMEM_LIMIT = 32 * 1024 * 1024
 EARLY_ROWS = 448
+REP_ORDER = (3, 6, 0, 5, 7, 1, 4, 2)
+FSDP_ORDER = (
+    61, 7, 0, 62, 39, 24, 40, 32, 53, 34, 3, 41, 51, 63, 6, 21,
+    43, 14, 38, 49, 30, 19, 23, 37, 55, 28, 58, 17, 29, 36, 52, 18,
+    22, 54, 57, 50, 5, 56, 31, 27, 60, 12, 2, 8, 48, 4, 46, 44,
+    33, 47, 26, 13, 11, 1, 25, 16, 59, 15, 45, 42, 20, 35, 9, 10,
+)
 
 
 def multiply(first, second):
@@ -54,10 +63,12 @@
 
 
 def block_kernel(
-    choice, gradient_ref, left_own, right_own, lent_early, lent_late,
+    order, choice, shares_ref, left_own, right_own, lent_early, lent_late,
     update_out, left_out, right_out, gradient_out,
-    left_old, right_old, left_new, right_new, update, old_sems, out_sems, update_sems,
+    left_old, right_old, left_new, right_new, gradient_ref, update,
+    old_sems, out_sems, update_sems,
 ):
+    rows = shares_ref.shape[1]
     lent, slot = choice[0], choice[1]
     width = left_old.shape[0]
     early = lent_early.shape[0]
@@ -82,6 +93,8 @@
         ).start()
         pltpu.make_async_copy(right_own.at[slot], right_old, old_sems.at[2]).start()
 
+    for number, place in enumerate(order):
+        gradient_ref[place * rows : (place + 1) * rows, :] = shares_ref[number]
     keep_gradient = pltpu.make_async_copy(gradient_ref, gradient_out, out_sems.at[2])
     keep_gradient.start()
     pltpu.make_async_copy(lent_early, left_old.at[:early], old_sems.at[0]).wait()
@@ -108,12 +121,15 @@
     raw_norm = jnp.sqrt(jnp.sum(raw_update * raw_update))
     scale = grad_norm / (raw_norm + 1e-06)
     sends = []
-    part = width // update_sems.shape[0]
+    part = len(order) // update_sems.shape[0]
     for number in range(update_sems.shape[0]):
-        rows = slice(number * part, (number + 1) * part)
-        update[rows, :] = (raw_update[rows, :] * scale).astype(jnp.bfloat16)
+        shares = slice(number * part, (number + 1) * part)
+        for share in range(number * part, (number + 1) * part):
+            place = order[share]
+            piece = raw_update[place * rows : (place + 1) * rows, :]
+            update[share] = (piece * scale).astype(jnp.bfloat16)
         send = pltpu.make_async_copy(
-            update.at[rows], update_out.at[rows], update_sems.at[number]
+            update.at[shares], update_out.at[shares], update_sems.at[number]
         )
         send.start()
         sends.append(send)
@@ -121,12 +137,14 @@
         send.wait()
 
 
-def work_on_block(choice, gradient, left_state, right_state, lent_early, lent_late):
-    width = gradient.shape[0]
+def work_on_block(
+    order, choice, shares, left_state, right_state, lent_early, lent_late
+):
+    width = shares.shape[2]
     square = pltpu.HBM((width, width), jnp.bfloat16)
     return pl.pallas_call(
-        block_kernel,
-        out_shape=(square,) * 4,
+        functools.partial(block_kernel, order),
+        out_shape=(pltpu.HBM(shares.shape, jnp.bfloat16),) + (square,) * 3,
         in_specs=[
             pl.BlockSpec(memory_space=pltpu.SMEM),
             pl.BlockSpec(memory_space=pltpu.VMEM),
@@ -134,13 +152,14 @@
         + [pl.BlockSpec(memory_space=pl.ANY)] * 4,
         out_specs=[pl.BlockSpec(memory_space=pltpu.HBM)] * 4,
         scratch_shapes=[pltpu.VMEM((width, width), jnp.bfloat16)] * 5
+        + [pltpu.VMEM(shares.shape, jnp.bfloat16)]
         + [pltpu.SemaphoreType.DMA((3,)), pltpu.SemaphoreType.DMA((3,)), pltpu.SemaphoreType.DMA((4,))],
         compiler_params=pltpu.CompilerParams(vmem_limit_bytes=VMEM_LIMIT),
         cost_estimate=pl.CostEstimate(
             flops=24 * width**3, bytes_accessed=12 * width**2, transcendentals=0
         ),
         name="block_step",
-    )(choice, gradient, left_state, right_state, lent_early, lent_late)
+    )(choice, shares, left_state, right_state, lent_early, lent_late)
 
 
 def settle_kernel(
@@ -269,6 +288,13 @@
     )(left_state, right_state)
 
 
+def exchange_order(order, count):
+    if len(order) != count:
+        order = tuple(range(count))
+    places = [order.index(device) for device in range(count)]
+    return [list(order)], places
+
+
 def pick(array, order):
     return array.at[order].get(mode="promise_in_bounds", unique_indices=True)
 
@@ -289,38 +315,51 @@
     lent_early = lax.ppermute(left_state[1, :early], "fsdp", swap)
     lent_late = lax.ppermute(late_loan(left_state, right_state, early), "fsdp", swap)
 
+    rep_groups, rep_place = exchange_order(REP_ORDER, rep_count)
+    fsdp_groups, fsdp_place = exchange_order(FSDP_ORDER, fsdp_count)
     owner_table = block_owner.reshape(rep_count, held_blocks)
     owner_column = owner_table // slot_count % rep_count
     before = positions[None, :] < positions[:, None]
 
     my_column = lax.dynamic_index_in_dim(owner_column, group_index, 0, keepdims=False)
     alike = (my_column[:, None] == my_column[None, :]) & before
-    my_order = my_column * column_share + jnp.sum(alike.astype(jnp.int32), axis=1)
+    my_place = sum(jnp.where(my_column == c, rep_place[c], 0) for c in range(rep_count))
+    my_order = my_place * column_share + jnp.sum(alike.astype(jnp.int32), axis=1)
     my_picked = jnp.sum(
         jnp.where(my_order[None, :] == positions[:, None], positions[None, :], 0), axis=1
     )
     arrived = lax.all_to_all(
         pick(grads, my_picked),
         "rep", split_axis=0, concat_axis=0, tiled=True,
-    )
-
-    mine = owner_column == group_index
+        axis_index_groups=rep_groups,
+    )
+
+    arrival_table = jnp.stack([owner_table[group] for group in rep_groups[0]])
+    mine = arrival_table // slot_count % rep_count == group_index
     rank = jnp.sum((mine[:, None, :] & before[None]).astype(jnp.int32), axis=2)
     shares = jnp.arange(column_share, dtype=jnp.int32)
     taken = mine[:, None, :] & (rank[:, None, :] == shares[None, :, None])
-    entry_owner = jnp.sum(jnp.where(taken, owner_table[:, None, :], 0), axis=2).reshape(-1)
+    entry_owner = jnp.sum(jnp.where(taken, arrival_table[:, None, :], 0), axis=2).reshape(-1)
 
     sibling = jnp.any(entry_owner[None, :] == entry_owner[:, None] - 1, axis=1)
     second = (entry_owner % slot_count == 1) & sibling
     owner_place = entry_owner // (slot_count * rep_count)
     worker = jnp.where(second, owner_place ^ half, owner_place)
+    worker_place = jnp.sum(
+        jnp.where(
+            worker[:, None] == jnp.array(fsdp_groups[0], jnp.int32)[None, :],
+            positions[None, :], 0,
+        ),
+        axis=1,
+    )
     source_entry = jnp.sum(
-        jnp.where(worker[None, :] == positions[:, None], positions[None, :], 0), axis=1
+        jnp.where(worker_place[None, :] == positions[:, None], positions[None, :], 0), axis=1
     )
     gradient = lax.all_to_all(
         reorder(arrived, source_entry, lent_early),
         "fsdp", split_axis=0, concat_axis=0, tiled=True,
-    ).reshape(fsdp_count * shard_rows, block_width)
+        axis_index_groups=fsdp_groups,
+    )
 
     first_slot = (place_index * rep_count + group_index) * slot_count
     owns_first = jnp.any(entry_owner == first_slot)
@@ -328,19 +367,21 @@
     lent = ~(owns_first | owns_second)
     choice = jnp.stack([lent, ~owns_first, owns_first, owns_second]).astype(jnp.int32)
     update_block, left_done, right_done, gradient = work_on_block(
-        choice, gradient, left_state, right_state, lent_early, lent_late
+        fsdp_groups[0], choice, gradient, left_state, right_state, lent_early, lent_late
     )
 
     returned_rows = lax.all_to_all(
-        update_block.reshape(fsdp_count, shard_rows, block_width),
+        update_block,
         "fsdp", split_axis=0, concat_axis=0, tiled=True,
+        axis_index_groups=fsdp_groups,
     )
     gradient_back = lax.ppermute(gradient, "fsdp", swap)
     left_new, right_new = settle(
         choice, gradient_back, left_state, right_state, left_done, right_done
     )
     at_home = lax.all_to_all(
-        reorder(returned_rows, worker), "rep", split_axis=0, concat_axis=0, tiled=True
+        reorder(returned_rows, worker_place), "rep", split_axis=0, concat_axis=0, tiled=True,
+        axis_index_groups=rep_groups
     )
     update = reorder(at_home, my_order)
     return (update, left_new, right_new)

time: 137 us -> 134 us (0.978)
  waiting for transfers between devices: 57.1 us -> 52.6 us
    all_to_all x2, starting transfers between devices: 16 us -> 18.3 us  [the longest x1 9.57 us: local(): lax.all_to_all(update_block, 'fsdp', split_axis=0, concat_axis=0, tiled=T...]
    all_to_all x1, starting transfers between devices: 15 us -> 17.3 us  [local(): lax.all_to_all(reorder(arrived, source_entry, lent_early), 'fsdp', split_...]
    all_to_all x1, waiting for transfers between devices: 8.6 us -> 6.42 us  [local(): lax.all_to_all(pick(grads, my_picked), 'rep', split_axis=0, concat_axis=0...]
    all_to_all x1, waiting for transfers between devices: 6.85 us -> 4.77 us  [local(): lax.all_to_all(reorder(arrived, source_entry, lent_early), 'fsdp', split_...]
    all_to_all x2, waiting for transfers between devices: 28.7 us -> 27 us  [the longest x1 22.7 us: local(): lax.all_to_all(update_block, 'fsdp', split_axis=0, concat_axis=0, tiled=T...]
    ppermute x1, waiting for transfers between devices: 12.9 us -> 14.5 us  [local(): lax.ppermute(late_loan(left_state, right_state, early), 'fsdp', swap)]
    ppermute x1, starting transfers between devices: 4.52 us -> 3.1 us  [local(): lax.ppermute(late_loan(left_state, right_state, early), 'fsdp', swap)]
    ppermute x1, starting transfers between devices: 4.52 us -> 3.09 us  [local(): gradient_back = lax.ppermute(gradient, 'fsdp', swap)]
  transfers between devices with their start and end apart: 7 -> 7, of which waited for: 5 -> 5; matrix products, arithmetic and copies ran while one was open for 3% -> 4% of each run, Pallas kernels for 3% -> 3%
where the time goes in v4:
time: 134 us; the launch traced here: 133 us
  starting transfers between devices  53.2 us (40%)
  waiting for transfers between devices  52.6 us (39%)
  Pallas kernels  14.6 us (11%)
  local copies, waits for them, and re-layouts  6.94 us (5%)
  other arithmetic  3.22 us (2%)
  between operations  2.74 us (2%)
    all_to_all x1, waiting for transfers between devices, local(): lax.all_to_all(update_block, 'fsdp', split_axis=0, concat_axis=0, tiled=T...  22.7 us
    all_to_all x1, starting transfers between devices, local(): lax.all_to_all(reorder(arrived, source_entry, lent_early), 'fsdp', split_...  17.3 us
    ppermute x1, waiting for transfers between devices, local(): lax.ppermute(late_loan(left_state, right_state, early), 'fsdp', swap)  14.5 us
    all_to_all x1, starting transfers between devices, local(): lax.all_to_all(update_block, 'fsdp', split_axis=0, concat_axis=0, tiled=T...  9.57 us
    all_to_all x1, starting transfers between devices, local(): lax.all_to_all(reorder(returned_rows, worker_place), 'rep', split_axis=0,...  8.76 us
    pallas_call x1, Pallas kernels, work_on_block(): pl.pallas_call(functools.partial(block_kernel, order), out_shape=(pltpu.H...  7.55 us
    all_to_all x1, waiting for transfers between devices, local(): lax.all_to_all(pick(grads, my_picked), 'rep', split_axis=0, concat_axis=0...  6.42 us
    all_to_all x1, starting transfers between devices, local(): lax.all_to_all(pick(grads, my_picked), 'rep', split_axis=0, concat_axis=0...  5.8 us
  transfers between devices with their start and end apart: 7, of which 5 were waited for; matrix products, arithmetic and copies ran while one was open for 4% of the time, Pallas kernels for 3%

profile of v4, /device:TPU:1, one launch (start us, length us, event | category | flops | bytes accessed | tf_op | source)
XLA Modules:
  0.0 133.3 jit_solution(13680341696237754104)
XLA Ops:
  0.6 1.9 %slice_bitcast_fusion = bf16[448,512]{1,0:T(8,128)(2,1)} fusion(bf16[2,512,512]{2,1,0:T(8,128)(2,1)} %left_own.5), kind=kLoop, calls=%fused_computation.1 | loop fusion | bytes 917504 | tf_op jit(solution)/shard_map/squeeze | solution.py:315
  2.5 5.6 %collective-permute-start = (bf16[448,512]{1,0:T(8,128)(2,1)}, bf16[448,512]{1,0:T(8,128)(2,1)}, u32[]{:S(2)}, u32[]{:S(2)}) collective-permute-start(bf16[448,512]{1,0:T(8,128)(2,1)} %slice_bitcast_fusion), channel_id=1, source_target_pairs={{0,256},{8,264},{16,272},{24,280},{32,288},{40,296},{48,304},{56,3... | collective-permute-start | bytes 1376264 | tf_op jit(solution)/shard_map/ppermute | solution.py:315
  8.2 0.7 copy-done.5
  9.3 1.4 %gather_fusion = bf16[64,8,512]{2,1,0:T(8,128)(2,1)} fusion(bf16[64,8,512]{2,1,0:T(8,128)(2,1)S(1)} %copy-done, s32[1024]{0:T(1024)S(1)} %pad_clamp_fusion), kind=kCustom, calls=%fused_computation | custom fusion | bytes 1048832 | tf_op jit(solution)/shard_map/gather | solution.py:299
  10.7 5.8 %all-to-all-start = ((bf16[64,8,512]{2,1,0:T(8,128)(2,1)}), bf16[64,8,512]{2,1,0:T(8,128)(2,1)S(1)}, u32[]{:S(2)}, u32[]{:S(2)}) async-start(bf16[64,8,512]{2,1,0:T(8,128)(2,1)} %gather_fusion), calls=%async_computation | async-start | bytes 1048576 | tf_op jit(solution)/shard_map/all_to_all | solution.py:331
  18.4 6.4 %all-to-all-done.source = bf16[64,8,512]{2,1,0:T(8,128)(2,1)S(1)} async-done(((bf16[64,8,512]{2,1,0:T(8,128)(2,1)}), bf16[64,8,512]{2,1,0:T(8,128)(2,1)S(1)}, u32[]{:S(2)}, u32[]{:S(2)}) %all-to-all-start) | async-done | bytes 524320 | tf_op jit(solution)/shard_map/all_to_all | solution.py:331
  24.8 1.4 %reorder.3 = bf16[64,8,512]{2,1,0:T(8,128)(2,1)} custom-call(s32[64]{0:T(128)S(1)} %select_reduce_fusion.1.order, bf16[64,8,512]{2,1,0:T(8,128)(2,1)S(1)} %all-to-all-done.source, bf16[448,512]{1,0:T(8,128)(2,1)} %collective-permute-done.rest_0_.lent_early), custom_call_target="tpu_custom_call" | custom-call | tf_op jit(solution)/shard_map/reorder/pallas_call | solution.py:247
  26.2 17.3 %all-to-all-start.1 = ((bf16[64,8,512]{2,1,0:T(8,128)(2,1)}), bf16[64,8,512]{2,1,0:T(8,128)(2,1)S(1)}, u32[]{:S(2)}, u32[]{:S(2)}) async-start(bf16[64,8,512]{2,1,0:T(8,128)(2,1)} %reorder.3), calls=%async_computation.1 | async-start | bytes 1048576 | tf_op jit(solution)/shard_map/all_to_all | solution.py:358
  43.5 1.0 late_loan.1
  44.5 3.1 %collective-permute-start.1 = (bf16[576,512]{1,0:T(8,128)(2,1)}, bf16[576,512]{1,0:T(8,128)(2,1)}, u32[]{:S(2)}, u32[]{:S(2)}) collective-permute-start(bf16[576,512]{1,0:T(8,128)(2,1)} %late_loan.1), channel_id=1, source_target_pairs={{0,256},{8,264},{16,272},{24,280},{32,288},{40,296},{48,304},{56,3... | collective-permute-start | bytes 1769480 | tf_op jit(solution)/shard_map/ppermute | solution.py:316
  50.1 1.3 add_convert_fusion.choice
  51.3 14.5 %collective-permute-done.1.lent_late = bf16[576,512]{1,0:T(8,128)(2,1)} collective-permute-done((bf16[576,512]{1,0:T(8,128)(2,1)}, bf16[576,512]{1,0:T(8,128)(2,1)}, u32[]{:S(2)}, u32[]{:S(2)}) %collective-permute-start.1) | collective-permute-done | bytes 589856 | tf_op jit(solution)/shard_map/ppermute | solution.py:316
  65.8 4.8 %all-to-all-done.1.shares_ref = bf16[64,8,512]{2,1,0:T(8,128)(2,1)S(1)} async-done(((bf16[64,8,512]{2,1,0:T(8,128)(2,1)}), bf16[64,8,512]{2,1,0:T(8,128)(2,1)S(1)}, u32[]{:S(2)}, u32[]{:S(2)}) %all-to-all-start.1) | async-done | bytes 524320 | tf_op jit(solution)/shard_map/all_to_all | solution.py:358
  70.6 7.5 %block_step.1 = (bf16[64,8,512]{2,1,0:T(8,128)(2,1)}, bf16[512,512]{1,0:T(8,128)(2,1)}, bf16[512,512]{1,0:T(8,128)(2,1)}, bf16[512,512]{1,0:T(8,128)(2,1)}) custom-call(s32[4]{0:T(128)S(1)} %add_convert_fusion.choice, bf16[64,8,512]{2,1,0:T(8,128)(2,1)S(1)} %all-to-all-done.1.shares_ref, bf16[2,512,512]{2,1,0:T(8,128)(2,1)S(1)} %copy-done.1, ...), custom_call_target="tpu_custom_call" | custom-call | flops 3221225472 | bytes 3145728 | tf_op jit(solution)/shard_map/block_step/pallas_call | solution.py:145
  78.1 9.6 %all-to-all-start.2 = ((bf16[64,8,512]{2,1,0:T(8,128)(2,1)}), bf16[64,8,512]{2,1,0:T(8,128)(2,1)S(1)}, u32[]{:S(2)}, u32[]{:S(2)}) async-start(bf16[64,8,512]{2,1,0:T(8,128)(2,1)} %get-tuple-element.9), calls=%async_computation.2 | async-start | bytes 1048576 | tf_op jit(solution)/shard_map/all_to_all | solution.py:373
  87.7 3.1 %collective-permute-start.2 = (bf16[512,512]{1,0:T(8,128)(2,1)}, bf16[512,512]{1,0:T(8,128)(2,1)}, u32[]{:S(2)}, u32[]{:S(2)}) collective-permute-start(bf16[512,512]{1,0:T(8,128)(2,1)} %get-tuple-element.10), channel_id=1, source_target_pairs={{0,256},{8,264},{16,272},{24,280},{32,288},{40,296},{48,304},{56,3... | collective-permute-start | bytes 1572872 | tf_op jit(solution)/shard_map/ppermute | solution.py:378
  90.8 22.7 %all-to-all-done.2.source = bf16[64,8,512]{2,1,0:T(8,128)(2,1)S(1)} async-done(((bf16[64,8,512]{2,1,0:T(8,128)(2,1)}), bf16[64,8,512]{2,1,0:T(8,128)(2,1)S(1)}, u32[]{:S(2)}, u32[]{:S(2)}) %all-to-all-start.2) | async-done | bytes 524320 | tf_op jit(solution)/shard_map/all_to_all | solution.py:373
  113.5 1.4 %reorder.4 = bf16[64,8,512]{2,1,0:T(8,128)(2,1)} custom-call(s32[64]{0:T(128)S(1)} %select_reduce_fusion.2.order, bf16[64,8,512]{2,1,0:T(8,128)(2,1)S(1)} %all-to-all-done.2.source), custom_call_target="tpu_custom_call" | custom-call | tf_op jit(solution)/shard_map/reorder/pallas_call | solution.py:247
  114.9 8.8 %all-to-all-start.3 = ((bf16[64,8,512]{2,1,0:T(8,128)(2,1)}), bf16[64,8,512]{2,1,0:T(8,128)(2,1)S(1)}, u32[]{:S(2)}, u32[]{:S(2)}) async-start(bf16[64,8,512]{2,1,0:T(8,128)(2,1)} %reorder.4), calls=%async_computation.3 | async-start | bytes 1048576 | tf_op jit(solution)/shard_map/all_to_all | solution.py:382
  123.7 1.0 copy-done.3
  124.8 1.0 copy-done.4
  125.8 1.9 %settle_slots.1 = (bf16[2,512,512]{2,1,0:T(8,128)(2,1)}, bf16[2,512,512]{2,1,0:T(8,128)(2,1)}) custom-call(s32[4]{0:T(128)S(1)} %add_convert_fusion.choice, bf16[512,512]{1,0:T(8,128)(2,1)} %collective-permute-done.2.gradient_back, bf16[2,512,512]{2,1,0:T(8,128)(2,1)S(1)} %copy-done.1, bf16[2,512,512]{2,1,0:T(8,128)(2,1)S(1)} %copy-done.2, ...), custom_call_target="tpu_custom_call" | custom-call | flops 536870912 | bytes 4194304 | tf_op jit(solution)/shard_map/settle_slots/pallas_call | solution.py:219
  127.7 4.3 %all-to-all-done.3.source = bf16[64,8,512]{2,1,0:T(8,128)(2,1)S(1)} async-done(((bf16[64,8,512]{2,1,0:T(8,128)(2,1)}), bf16[64,8,512]{2,1,0:T(8,128)(2,1)S(1)}, u32[]{:S(2)}, u32[]{:S(2)}) %all-to-all-start.3) | async-done | bytes 524320 | tf_op jit(solution)/shard_map/all_to_all | solution.py:382
  132.0 1.4 %reorder.5 = bf16[64,8,512]{2,1,0:T(8,128)(2,1)} custom-call(s32[64]{0:T(128)S(1)} %fusion.15.order, bf16[64,8,512]{2,1,0:T(8,128)(2,1)S(1)} %all-to-all-done.3.source), custom_call_target="tpu_custom_call" | custom-call | tf_op jit(solution)/shard_map/reorder/pallas_call | solution.py:247
  (35 shorter events, 2.9 us)
Async XLA Ops:
  0.6 8.7 %copy-start = (bf16[64,8,512]{2,1,0:T(8,128)(2,1)S(1)}, bf16[64,8,512]{2,1,0:T(8,128)(2,1)}, u32[]{:S(2)}) copy-start(bf16[64,8,512]{2,1,0:T(8,128)(2,1)} %param.5) | copy-start | bytes 1572868
  2.5 15.8 %collective-permute-start = (bf16[448,512]{1,0:T(8,128)(2,1)}, bf16[448,512]{1,0:T(8,128)(2,1)}, u32[]{:S(2)}, u32[]{:S(2)}) collective-permute-start(bf16[448,512]{1,0:T(8,128)(2,1)} %slice_bitcast_fusion), channel_id=1, source_target_pairs={{0,256},{8,264},{16,272},{24,280},{32,288},{40,296},{48,304},{56,3... | collective-permute-start | bytes 1376264 | tf_op jit(solution)/shard_map/ppermute | solution.py:315
  8.2 0.7 copy-start.5
  10.7 14.1 %all-to-all-start = ((bf16[64,8,512]{2,1,0:T(8,128)(2,1)}), bf16[64,8,512]{2,1,0:T(8,128)(2,1)S(1)}, u32[]{:S(2)}, u32[]{:S(2)}) async-start(bf16[64,8,512]{2,1,0:T(8,128)(2,1)} %gather_fusion), calls=%async_computation | async-start | bytes 1048576 | tf_op jit(solution)/shard_map/all_to_all | solution.py:331
  17.4 0.7 copy-start.6
  18.3 25.1 %copy-start.1 = (bf16[2,512,512]{2,1,0:T(8,128)(2,1)S(1)}, bf16[2,512,512]{2,1,0:T(8,128)(2,1)}, u32[]{:S(2)}) copy-start(bf16[2,512,512]{2,1,0:T(8,128)(2,1)} %left_own.5) | copy-start | bytes 3145732
  18.3 25.1 %copy-start.2 = (bf16[2,512,512]{2,1,0:T(8,128)(2,1)S(1)}, bf16[2,512,512]{2,1,0:T(8,128)(2,1)}, u32[]{:S(2)}) copy-start(bf16[2,512,512]{2,1,0:T(8,128)(2,1)} %right_own.5) | copy-start | bytes 3145732
  26.2 44.4 %all-to-all-start.1 = ((bf16[64,8,512]{2,1,0:T(8,128)(2,1)}), bf16[64,8,512]{2,1,0:T(8,128)(2,1)S(1)}, u32[]{:S(2)}, u32[]{:S(2)}) async-start(bf16[64,8,512]{2,1,0:T(8,128)(2,1)} %reorder.3), calls=%async_computation.1 | async-start | bytes 1048576 | tf_op jit(solution)/shard_map/all_to_all | solution.py:358
  44.5 21.3 %collective-permute-start.1 = (bf16[576,512]{1,0:T(8,128)(2,1)}, bf16[576,512]{1,0:T(8,128)(2,1)}, u32[]{:S(2)}, u32[]{:S(2)}) collective-permute-start(bf16[576,512]{1,0:T(8,128)(2,1)} %late_loan.1), channel_id=1, source_target_pairs={{0,256},{8,264},{16,272},{24,280},{32,288},{40,296},{48,304},{56,3... | collective-permute-start | bytes 1769480 | tf_op jit(solution)/shard_map/ppermute | solution.py:316
  78.1 35.4 %all-to-all-start.2 = ((bf16[64,8,512]{2,1,0:T(8,128)(2,1)}), bf16[64,8,512]{2,1,0:T(8,128)(2,1)S(1)}, u32[]{:S(2)}, u32[]{:S(2)}) async-start(bf16[64,8,512]{2,1,0:T(8,128)(2,1)} %get-tuple-element.9), calls=%async_computation.2 | async-start | bytes 1048576 | tf_op jit(solution)/shard_map/all_to_all | solution.py:373
  87.7 36.0 %collective-permute-start.2 = (bf16[512,512]{1,0:T(8,128)(2,1)}, bf16[512,512]{1,0:T(8,128)(2,1)}, u32[]{:S(2)}, u32[]{:S(2)}) collective-permute-start(bf16[512,512]{1,0:T(8,128)(2,1)} %get-tuple-element.10), channel_id=1, source_target_pairs={{0,256},{8,264},{16,272},{24,280},{32,288},{40,296},{48,304},{56,3... | collective-permute-start | bytes 1572872 | tf_op jit(solution)/shard_map/ppermute | solution.py:378
  114.9 17.0 %all-to-all-start.3 = ((bf16[64,8,512]{2,1,0:T(8,128)(2,1)}), bf16[64,8,512]{2,1,0:T(8,128)(2,1)S(1)}, u32[]{:S(2)}, u32[]{:S(2)}) async-start(bf16[64,8,512]{2,1,0:T(8,128)(2,1)} %reorder.4), calls=%async_computation.3 | async-start | bytes 1048576 | tf_op jit(solution)/shard_map/all_to_all | solution.py:382
  123.7 1.0 copy-start.3
  124.8 1.0 copy-start.4

commit v5 on v4

--- a/solution.py
+++ b/solution.py
@@ -12,12 +12,7 @@
 VMEM_LIMIT = 32 * 1024 * 1024
 EARLY_ROWS = 448
 REP_ORDER = (3, 6, 0, 5, 7, 1, 4, 2)
-FSDP_ORDER = (
-    61, 7, 0, 62, 39, 24, 40, 32, 53, 34, 3, 41, 51, 63, 6, 21,
-    43, 14, 38, 49, 30, 19, 23, 37, 55, 28, 58, 17, 29, 36, 52, 18,
-    22, 54, 57, 50, 5, 56, 31, 27, 60, 12, 2, 8, 48, 4, 46, 44,
-    33, 47, 26, 13, 11, 1, 25, 16, 59, 15, 45, 42, 20, 35, 9, 10,
-)
+FSDP_FIRST = 43
 
 
 def multiply(first, second):
@@ -316,7 +311,9 @@
     lent_late = lax.ppermute(late_loan(left_state, right_state, early), "fsdp", swap)
 
     rep_groups, rep_place = exchange_order(REP_ORDER, rep_count)
-    fsdp_groups, fsdp_place = exchange_order(FSDP_ORDER, fsdp_count)
+    fsdp_order = list(range(fsdp_count))
+    first = FSDP_FIRST % fsdp_count
+    fsdp_order[0], fsdp_order[first] = first, 0
     owner_table = block_owner.reshape(rep_count, held_blocks)
     owner_column = owner_table // slot_count % rep_count
     before = positions[None, :] < positions[:, None]
@@ -345,12 +342,8 @@
     second = (entry_owner % slot_count == 1) & sibling
     owner_place = entry_owner // (slot_count * rep_count)
     worker = jnp.where(second, owner_place ^ half, owner_place)
-    worker_place = jnp.sum(
-        jnp.where(
-            worker[:, None] == jnp.array(fsdp_groups[0], jnp.int32)[None, :],
-            positions[None, :], 0,
-        ),
-        axis=1,
+    worker_place = jnp.where(
+        worker == 0, first, jnp.where(worker == first, 0, worker)
     )
     source_entry = jnp.sum(
         jnp.where(worker_place[None, :] == positions[:, None], positions[None, :], 0), axis=1
@@ -358,7 +351,7 @@
     gradient = lax.all_to_all(
         reorder(arrived, source_entry, lent_early),
         "fsdp", split_axis=0, concat_axis=0, tiled=True,
-        axis_index_groups=fsdp_groups,
+        axis_index_groups=[fsdp_order],
     )
 
     first_slot = (place_index * rep_count + group_index) * slot_count
@@ -367,13 +360,13 @@
     lent = ~(owns_first | owns_second)
     choice = jnp.stack([lent, ~owns_first, owns_first, owns_second]).astype(jnp.int32)
     update_block, left_done, right_done, gradient = work_on_block(
-        fsdp_groups[0], choice, gradient, left_state, right_state, lent_early, lent_late
+        fsdp_order, choice, gradient, left_state, right_state, lent_early, lent_late
     )
 
     returned_rows = lax.all_to_all(
         update_block,
         "fsdp", split_axis=0, concat_axis=0, tiled=True,
-        axis_index_groups=fsdp_groups,
+        axis_index_groups=[fsdp_order],
     )
     gradient_back = lax.ppermute(gradient, "fsdp", swap)
     left_new, right_new = settle(

time: 134 us -> 130 us (0.970)
  waiting for transfers between devices: 52.6 us -> 46.8 us
  starting transfers between devices: 53.2 us -> 57.3 us
    all_to_all x1, starting transfers between devices: 9.57 us -> 14.8 us  [local(): lax.all_to_all(update_block, 'fsdp', split_axis=0, concat_axis=0, tiled=T...]
    all_to_all x1, waiting for transfers between devices: 4.77 us -> 0.47 us  [local(): lax.all_to_all(reorder(arrived, source_entry, lent_early), 'fsdp', split_...]
    all_to_all x1, waiting for transfers between devices: 22.7 us -> 19.2 us  [local(): lax.all_to_all(update_block, 'fsdp', split_axis=0, concat_axis=0, tiled=T...]
    unnamed x14 -> x12, local copies, waits for them, and re-layouts: 3.41 us -> 2.78 us
where the time goes in v5:
time: 130 us
  starting transfers between devices  57.3 us (44%)
  waiting for transfers between devices  46.8 us (36%)
  Pallas kernels  13.6 us (10%)
  local copies, waits for them, and re-layouts  6.3 us (5%)
  other arithmetic  3.04 us (2%)
  between operations  2.73 us (2%)
    all_to_all x1, waiting for transfers between devices, local(): lax.all_to_all(update_block, 'fsdp', split_axis=0, concat_axis=0, tiled=T...  19.2 us
    all_to_all x1, starting transfers between devices, local(): lax.all_to_all(reorder(arrived, source_entry, lent_early), 'fsdp', split_...  18.1 us
    ppermute x1, waiting for transfers between devices, local(): lax.ppermute(late_loan(left_state, right_state, early), 'fsdp', swap)  15.6 us
    all_to_all x1, starting transfers between devices, local(): lax.all_to_all(update_block, 'fsdp', split_axis=0, concat_axis=0, tiled=T...  14.8 us
    all_to_all x1, starting transfers between devices, local(): lax.all_to_all(reorder(returned_rows, worker_place), 'rep', split_axis=0,...  8.7 us
    all_to_all x1, waiting for transfers between devices, local(): lax.all_to_all(pick(grads, my_picked), 'rep', split_axis=0, concat_axis=0...  7.24 us
    pallas_call x1, Pallas kernels, work_on_block(): pl.pallas_call(functools.partial(block_kernel, order), out_shape=(pltpu.H...  6.59 us
    all_to_all x1, starting transfers between devices, local(): lax.all_to_all(pick(grads, my_picked), 'rep', split_axis=0, concat_axis=0...  5.8 us
  transfers between devices with their start and end apart: 7, of which 5 were waited for; matrix products, arithmetic and copies ran while one was open for 4% of the time, Pallas kernels for 3%

profile of v5, /device:TPU:1, one launch (start us, length us, event | category | flops | bytes accessed | tf_op | source)
XLA Modules:
  0.0 129.8 jit_solution(9708942661812250343)
XLA Ops:
  0.6 1.9 %slice_bitcast_fusion = bf16[448,512]{1,0:T(8,128)(2,1)} fusion(bf16[2,512,512]{2,1,0:T(8,128)(2,1)} %left_own.5), kind=kLoop, calls=%fused_computation.1 | loop fusion | bytes 917504 | tf_op jit(solution)/shard_map/squeeze | solution.py:310
  2.5 5.6 %collective-permute-start = (bf16[448,512]{1,0:T(8,128)(2,1)}, bf16[448,512]{1,0:T(8,128)(2,1)}, u32[]{:S(2)}, u32[]{:S(2)}) collective-permute-start(bf16[448,512]{1,0:T(8,128)(2,1)} %slice_bitcast_fusion), channel_id=1, source_target_pairs={{0,256},{8,264},{16,272},{24,280},{32,288},{40,296},{48,304},{56,3... | collective-permute-start | bytes 1376264 | tf_op jit(solution)/shard_map/ppermute | solution.py:310
  8.2 0.7 copy-done.5
  9.3 1.4 %gather_fusion = bf16[64,8,512]{2,1,0:T(8,128)(2,1)} fusion(bf16[64,8,512]{2,1,0:T(8,128)(2,1)S(1)} %copy-done, s32[1024]{0:T(1024)S(1)} %pad_clamp_fusion), kind=kCustom, calls=%fused_computation | custom fusion | bytes 1048832 | tf_op jit(solution)/shard_map/gather | solution.py:294
  10.7 5.8 %all-to-all-start = ((bf16[64,8,512]{2,1,0:T(8,128)(2,1)}), bf16[64,8,512]{2,1,0:T(8,128)(2,1)S(1)}, u32[]{:S(2)}, u32[]{:S(2)}) async-start(bf16[64,8,512]{2,1,0:T(8,128)(2,1)} %gather_fusion), calls=%async_computation | async-start | bytes 1048576 | tf_op jit(solution)/shard_map/all_to_all | solution.py:328
  17.5 7.2 %all-to-all-done.source = bf16[64,8,512]{2,1,0:T(8,128)(2,1)S(1)} async-done(((bf16[64,8,512]{2,1,0:T(8,128)(2,1)}), bf16[64,8,512]{2,1,0:T(8,128)(2,1)S(1)}, u32[]{:S(2)}, u32[]{:S(2)}) %all-to-all-start) | async-done | bytes 524320 | tf_op jit(solution)/shard_map/all_to_all | solution.py:328
  24.8 1.4 %reorder.3 = bf16[64,8,512]{2,1,0:T(8,128)(2,1)} custom-call(s32[64]{0:T(128)S(1)} %select_reduce_fusion.1.order, bf16[64,8,512]{2,1,0:T(8,128)(2,1)S(1)} %all-to-all-done.source, bf16[448,512]{1,0:T(8,128)(2,1)} %collective-permute-done.rest_0_.lent_early), custom_call_target="tpu_custom_call" | custom-call | tf_op jit(solution)/shard_map/reorder/pallas_call | solution.py:242
  26.2 18.1 %all-to-all-start.1 = ((bf16[64,8,512]{2,1,0:T(8,128)(2,1)}), bf16[64,8,512]{2,1,0:T(8,128)(2,1)S(1)}, u32[]{:S(2)}, u32[]{:S(2)}) async-start(bf16[64,8,512]{2,1,0:T(8,128)(2,1)} %reorder.3), calls=%async_computation.1 | async-start | bytes 1048576 | tf_op jit(solution)/shard_map/all_to_all | solution.py:351
  44.3 1.0 late_loan.1
  45.3 2.1 %collective-permute-start.1 = (bf16[576,512]{1,0:T(8,128)(2,1)}, bf16[576,512]{1,0:T(8,128)(2,1)}, u32[]{:S(2)}, u32[]{:S(2)}) collective-permute-start(bf16[576,512]{1,0:T(8,128)(2,1)} %late_loan.1), channel_id=1, source_target_pairs={{0,256},{8,264},{16,272},{24,280},{32,288},{40,296},{48,304},{56,3... | collective-permute-start | bytes 1769480 | tf_op jit(solution)/shard_map/ppermute | solution.py:311
  47.4 0.6 compare_reduce_fusion.2
  49.9 1.3 add_convert_fusion.choice
  51.2 15.6 %collective-permute-done.1.lent_late = bf16[576,512]{1,0:T(8,128)(2,1)} collective-permute-done((bf16[576,512]{1,0:T(8,128)(2,1)}, bf16[576,512]{1,0:T(8,128)(2,1)}, u32[]{:S(2)}, u32[]{:S(2)}) %collective-permute-start.1) | collective-permute-done | bytes 589856 | tf_op jit(solution)/shard_map/ppermute | solution.py:311
  67.3 6.6 %block_step.1 = (bf16[64,8,512]{2,1,0:T(8,128)(2,1)}, bf16[512,512]{1,0:T(8,128)(2,1)}, bf16[512,512]{1,0:T(8,128)(2,1)}, bf16[512,512]{1,0:T(8,128)(2,1)}) custom-call(s32[4]{0:T(128)S(1)} %add_convert_fusion.choice, bf16[64,8,512]{2,1,0:T(8,128)(2,1)S(1)} %all-to-all-done.1.shares_ref, bf16[2,512,512]{2,1,0:T(8,128)(2,1)S(1)} %copy-done.1, ...), custom_call_target="tpu_custom_call" | custom-call | flops 3221225472 | bytes 3145728 | tf_op jit(solution)/shard_map/block_step/pallas_call | solution.py:140
  73.9 14.8 %all-to-all-start.2 = ((bf16[64,8,512]{2,1,0:T(8,128)(2,1)}), bf16[64,8,512]{2,1,0:T(8,128)(2,1)S(1)}, u32[]{:S(2)}, u32[]{:S(2)}) async-start(bf16[64,8,512]{2,1,0:T(8,128)(2,1)} %get-tuple-element.9), calls=%async_computation.2 | async-start | bytes 1048576 | tf_op jit(solution)/shard_map/all_to_all | solution.py:366
  88.7 2.1 %collective-permute-start.2 = (bf16[512,512]{1,0:T(8,128)(2,1)}, bf16[512,512]{1,0:T(8,128)(2,1)}, u32[]{:S(2)}, u32[]{:S(2)}) collective-permute-start(bf16[512,512]{1,0:T(8,128)(2,1)} %get-tuple-element.10), channel_id=1, source_target_pairs={{0,256},{8,264},{16,272},{24,280},{32,288},{40,296},{48,304},{56,3... | collective-permute-start | bytes 1572872 | tf_op jit(solution)/shard_map/ppermute | solution.py:371
  90.8 19.2 %all-to-all-done.2.source = bf16[64,8,512]{2,1,0:T(8,128)(2,1)S(1)} async-done(((bf16[64,8,512]{2,1,0:T(8,128)(2,1)}), bf16[64,8,512]{2,1,0:T(8,128)(2,1)S(1)}, u32[]{:S(2)}, u32[]{:S(2)}) %all-to-all-start.2) | async-done | bytes 524320 | tf_op jit(solution)/shard_map/all_to_all | solution.py:366
  110.0 1.4 %reorder.4 = bf16[64,8,512]{2,1,0:T(8,128)(2,1)} custom-call(s32[64]{0:T(128)S(1)} %compare_select_fusion.9.order, bf16[64,8,512]{2,1,0:T(8,128)(2,1)S(1)} %all-to-all-done.2.source), custom_call_target="tpu_custom_call" | custom-call | tf_op jit(solution)/shard_map/reorder/pallas_call | solution.py:242
  111.4 8.7 %all-to-all-start.3 = ((bf16[64,8,512]{2,1,0:T(8,128)(2,1)}), bf16[64,8,512]{2,1,0:T(8,128)(2,1)S(1)}, u32[]{:S(2)}, u32[]{:S(2)}) async-start(bf16[64,8,512]{2,1,0:T(8,128)(2,1)} %reorder.4), calls=%async_computation.3 | async-start | bytes 1048576 | tf_op jit(solution)/shard_map/all_to_all | solution.py:375
  120.1 1.0 copy-done.3
  121.2 1.0 copy-done.4
  122.2 1.9 %settle_slots.1 = (bf16[2,512,512]{2,1,0:T(8,128)(2,1)}, bf16[2,512,512]{2,1,0:T(8,128)(2,1)}) custom-call(s32[4]{0:T(128)S(1)} %add_convert_fusion.choice, bf16[512,512]{1,0:T(8,128)(2,1)} %collective-permute-done.2.gradient_back, bf16[2,512,512]{2,1,0:T(8,128)(2,1)S(1)} %copy-done.1, bf16[2,512,512]{2,1,0:T(8,128)(2,1)S(1)} %copy-done.2, ...), custom_call_target="tpu_custom_call" | custom-call | flops 536870912 | bytes 4194304 | tf_op jit(solution)/shard_map/settle_slots/pallas_call | solution.py:214
  124.1 4.3 %all-to-all-done.3.source = bf16[64,8,512]{2,1,0:T(8,128)(2,1)S(1)} async-done(((bf16[64,8,512]{2,1,0:T(8,128)(2,1)}), bf16[64,8,512]{2,1,0:T(8,128)(2,1)S(1)}, u32[]{:S(2)}, u32[]{:S(2)}) %all-to-all-start.3) | async-done | bytes 524320 | tf_op jit(solution)/shard_map/all_to_all | solution.py:375
  128.4 1.4 %reorder.5 = bf16[64,8,512]{2,1,0:T(8,128)(2,1)} custom-call(s32[64]{0:T(128)S(1)} %fusion.15.order, bf16[64,8,512]{2,1,0:T(8,128)(2,1)S(1)} %all-to-all-done.3.source), custom_call_target="tpu_custom_call" | custom-call | tf_op jit(solution)/shard_map/reorder/pallas_call | solution.py:242
  (32 shorter events, 1.9 us)
Async XLA Ops:
  0.6 8.7 %copy-start = (bf16[64,8,512]{2,1,0:T(8,128)(2,1)S(1)}, bf16[64,8,512]{2,1,0:T(8,128)(2,1)}, u32[]{:S(2)}) copy-start(bf16[64,8,512]{2,1,0:T(8,128)(2,1)} %param.4) | copy-start | bytes 1572868
  2.5 15.0 %collective-permute-start = (bf16[448,512]{1,0:T(8,128)(2,1)}, bf16[448,512]{1,0:T(8,128)(2,1)}, u32[]{:S(2)}, u32[]{:S(2)}) collective-permute-start(bf16[448,512]{1,0:T(8,128)(2,1)} %slice_bitcast_fusion), channel_id=1, source_target_pairs={{0,256},{8,264},{16,272},{24,280},{32,288},{40,296},{48,304},{56,3... | collective-permute-start | bytes 1376264 | tf_op jit(solution)/shard_map/ppermute | solution.py:310
  8.2 0.7 copy-start.5
  10.7 14.1 %all-to-all-start = ((bf16[64,8,512]{2,1,0:T(8,128)(2,1)}), bf16[64,8,512]{2,1,0:T(8,128)(2,1)S(1)}, u32[]{:S(2)}, u32[]{:S(2)}) async-start(bf16[64,8,512]{2,1,0:T(8,128)(2,1)} %gather_fusion), calls=%async_computation | async-start | bytes 1048576 | tf_op jit(solution)/shard_map/all_to_all | solution.py:328
  17.5 26.8 %copy-start.1 = (bf16[2,512,512]{2,1,0:T(8,128)(2,1)S(1)}, bf16[2,512,512]{2,1,0:T(8,128)(2,1)}, u32[]{:S(2)}) copy-start(bf16[2,512,512]{2,1,0:T(8,128)(2,1)} %left_own.5) | copy-start | bytes 3145732
  17.5 26.8 %copy-start.2 = (bf16[2,512,512]{2,1,0:T(8,128)(2,1)S(1)}, bf16[2,512,512]{2,1,0:T(8,128)(2,1)}, u32[]{:S(2)}) copy-start(bf16[2,512,512]{2,1,0:T(8,128)(2,1)} %right_own.5) | copy-start | bytes 3145732
  26.2 41.1 %all-to-all-start.1 = ((bf16[64,8,512]{2,1,0:T(8,128)(2,1)}), bf16[64,8,512]{2,1,0:T(8,128)(2,1)S(1)}, u32[]{:S(2)}, u32[]{:S(2)}) async-start(bf16[64,8,512]{2,1,0:T(8,128)(2,1)} %reorder.3), calls=%async_computation.1 | async-start | bytes 1048576 | tf_op jit(solution)/shard_map/all_to_all | solution.py:351
  45.3 21.5 %collective-permute-start.1 = (bf16[576,512]{1,0:T(8,128)(2,1)}, bf16[576,512]{1,0:T(8,128)(2,1)}, u32[]{:S(2)}, u32[]{:S(2)}) collective-permute-start(bf16[576,512]{1,0:T(8,128)(2,1)} %late_loan.1), channel_id=1, source_target_pairs={{0,256},{8,264},{16,272},{24,280},{32,288},{40,296},{48,304},{56,3... | collective-permute-start | bytes 1769480 | tf_op jit(solution)/shard_map/ppermute | solution.py:311
  73.9 36.1 %all-to-all-start.2 = ((bf16[64,8,512]{2,1,0:T(8,128)(2,1)}), bf16[64,8,512]{2,1,0:T(8,128)(2,1)S(1)}, u32[]{:S(2)}, u32[]{:S(2)}) async-start(bf16[64,8,512]{2,1,0:T(8,128)(2,1)} %get-tuple-element.9), calls=%async_computation.2 | async-start | bytes 1048576 | tf_op jit(solution)/shard_map/all_to_all | solution.py:366
  88.7 31.4 %collective-permute-start.2 = (bf16[512,512]{1,0:T(8,128)(2,1)}, bf16[512,512]{1,0:T(8,128)(2,1)}, u32[]{:S(2)}, u32[]{:S(2)}) collective-permute-start(bf16[512,512]{1,0:T(8,128)(2,1)} %get-tuple-element.10), channel_id=1, source_target_pairs={{0,256},{8,264},{16,272},{24,280},{32,288},{40,296},{48,304},{56,3... | collective-permute-start | bytes 1572872 | tf_op jit(solution)/shard_map/ppermute | solution.py:371
  111.4 17.0 %all-to-all-start.3 = ((bf16[64,8,512]{2,1,0:T(8,128)(2,1)}), bf16[64,8,512]{2,1,0:T(8,128)(2,1)S(1)}, u32[]{:S(2)}, u32[]{:S(2)}) async-start(bf16[64,8,512]{2,1,0:T(8,128)(2,1)} %reorder.4), calls=%async_computation.3 | async-start | bytes 1048576 | tf_op jit(solution)/shard_map/all_to_all | solution.py:375
  120.1 1.0 copy-start.3
  121.2 1.0 copy-start.4

commit v6 on v5

--- a/solution.py
+++ b/solution.py
@@ -11,8 +11,8 @@
 DECAY_RATE = 0.95
 VMEM_LIMIT = 32 * 1024 * 1024
 EARLY_ROWS = 448
-REP_ORDER = (3, 6, 0, 5, 7, 1, 4, 2)
-FSDP_FIRST = 43
+REP_ORDER = (5, 1, 0, 7, 3, 4, 2, 6)
+FSDP_FIRST = 42
 
 
 def multiply(first, second):

time: 130 us -> 130 us (level)
    all_to_all x1, starting transfers between devices: 8.7 us -> 5.46 us  [local(): lax.all_to_all(reorder(returned_rows, worker_place), 'rep', split_axis=0,...]
    all_to_all x1, waiting for transfers between devices: 19.2 us -> 21.5 us  [local(): lax.all_to_all(update_block, 'fsdp', split_axis=0, concat_axis=0, tiled=T...]
    all_to_all x1, starting transfers between devices: 5.8 us -> 7.27 us  [local(): lax.all_to_all(pick(grads, my_picked), 'rep', split_axis=0, concat_axis=0...]
where the time goes in v6:
time: 130 us
  starting transfers between devices  56.4 us (43%)
  waiting for transfers between devices  47.6 us (37%)
  Pallas kernels  13.6 us (10%)
  local copies, waits for them, and re-layouts  6.3 us (5%)
  other arithmetic  3.04 us (2%)
  between operations  2.73 us (2%)
    all_to_all x1, waiting for transfers between devices, local(): lax.all_to_all(update_block, 'fsdp', split_axis=0, concat_axis=0, tiled=T...  21.5 us
    all_to_all x1, starting transfers between devices, local(): lax.all_to_all(reorder(arrived, source_entry, lent_early), 'fsdp', split_...  18.5 us
    ppermute x1, waiting for transfers between devices, local(): lax.ppermute(late_loan(left_state, right_state, early), 'fsdp', swap)  16.4 us
    all_to_all x1, starting transfers between devices, local(): lax.all_to_all(update_block, 'fsdp', split_axis=0, concat_axis=0, tiled=T...  15.3 us
    all_to_all x1, starting transfers between devices, local(): lax.all_to_all(pick(grads, my_picked), 'rep', split_axis=0, concat_axis=0...  7.27 us
    pallas_call x1, Pallas kernels, work_on_block(): pl.pallas_call(functools.partial(block_kernel, order), out_shape=(pltpu.H...  6.58 us
    all_to_all x1, waiting for transfers between devices, local(): lax.all_to_all(pick(grads, my_picked), 'rep', split_axis=0, concat_axis=0...  6.03 us
    ppermute x1, starting transfers between devices, local(): lent_early = lax.ppermute(left_state[1, :early], 'fsdp', swap)  5.64 us
  transfers between devices with their start and end apart: 7, of which 5 were waited for; matrix products, arithmetic and copies ran while one was open for 4% of the time, Pallas kernels for 3%

profile of v6, /device:TPU:1, one launch (start us, length us, event | category | flops | bytes accessed | tf_op | source)
XLA Modules:
  0.0 129.7 jit_solution(2371243870691653509)
XLA Ops:
  0.6 1.9 %slice_bitcast_fusion = bf16[448,512]{1,0:T(8,128)(2,1)} fusion(bf16[2,512,512]{2,1,0:T(8,128)(2,1)} %left_own.5), kind=kLoop, calls=%fused_computation.1 | loop fusion | bytes 917504 | tf_op jit(solution)/shard_map/squeeze | solution.py:310
  2.5 5.6 %collective-permute-start = (bf16[448,512]{1,0:T(8,128)(2,1)}, bf16[448,512]{1,0:T(8,128)(2,1)}, u32[]{:S(2)}, u32[]{:S(2)}) collective-permute-start(bf16[448,512]{1,0:T(8,128)(2,1)} %slice_bitcast_fusion), channel_id=1, source_target_pairs={{0,256},{8,264},{16,272},{24,280},{32,288},{40,296},{48,304},{56,3... | collective-permute-start | bytes 1376264 | tf_op jit(solution)/shard_map/ppermute | solution.py:310
  8.2 0.7 copy-done.5
  9.3 1.4 %gather_fusion = bf16[64,8,512]{2,1,0:T(8,128)(2,1)} fusion(bf16[64,8,512]{2,1,0:T(8,128)(2,1)S(1)} %copy-done, s32[1024]{0:T(1024)S(1)} %pad_clamp_fusion), kind=kCustom, calls=%fused_computation | custom fusion | bytes 1048832 | tf_op jit(solution)/shard_map/gather | solution.py:294
  10.7 7.3 %all-to-all-start = ((bf16[64,8,512]{2,1,0:T(8,128)(2,1)}), bf16[64,8,512]{2,1,0:T(8,128)(2,1)S(1)}, u32[]{:S(2)}, u32[]{:S(2)}) async-start(bf16[64,8,512]{2,1,0:T(8,128)(2,1)} %gather_fusion), calls=%async_computation | async-start | bytes 1048576 | tf_op jit(solution)/shard_map/all_to_all | solution.py:328
  19.0 6.0 %all-to-all-done.source = bf16[64,8,512]{2,1,0:T(8,128)(2,1)S(1)} async-done(((bf16[64,8,512]{2,1,0:T(8,128)(2,1)}), bf16[64,8,512]{2,1,0:T(8,128)(2,1)S(1)}, u32[]{:S(2)}, u32[]{:S(2)}) %all-to-all-start) | async-done | bytes 524320 | tf_op jit(solution)/shard_map/all_to_all | solution.py:328
  25.0 1.4 %reorder.3 = bf16[64,8,512]{2,1,0:T(8,128)(2,1)} custom-call(s32[64]{0:T(128)S(1)} %select_reduce_fusion.1.order, bf16[64,8,512]{2,1,0:T(8,128)(2,1)S(1)} %all-to-all-done.source, bf16[448,512]{1,0:T(8,128)(2,1)} %collective-permute-done.rest_0_.lent_early), custom_call_target="tpu_custom_call" | custom-call | tf_op jit(solution)/shard_map/reorder/pallas_call | solution.py:242
  26.4 18.5 %all-to-all-start.1 = ((bf16[64,8,512]{2,1,0:T(8,128)(2,1)}), bf16[64,8,512]{2,1,0:T(8,128)(2,1)S(1)}, u32[]{:S(2)}, u32[]{:S(2)}) async-start(bf16[64,8,512]{2,1,0:T(8,128)(2,1)} %reorder.3), calls=%async_computation.1 | async-start | bytes 1048576 | tf_op jit(solution)/shard_map/all_to_all | solution.py:351
  45.0 1.0 late_loan.1
  45.9 2.1 %collective-permute-start.1 = (bf16[576,512]{1,0:T(8,128)(2,1)}, bf16[576,512]{1,0:T(8,128)(2,1)}, u32[]{:S(2)}, u32[]{:S(2)}) collective-permute-start(bf16[576,512]{1,0:T(8,128)(2,1)} %late_loan.1), channel_id=1, source_target_pairs={{0,256},{8,264},{16,272},{24,280},{32,288},{40,296},{48,304},{56,3... | collective-permute-start | bytes 1769480 | tf_op jit(solution)/shard_map/ppermute | solution.py:311
  48.1 0.6 compare_reduce_fusion.2
  50.6 1.3 add_convert_fusion.choice
  51.9 16.4 %collective-permute-done.1.lent_late = bf16[576,512]{1,0:T(8,128)(2,1)} collective-permute-done((bf16[576,512]{1,0:T(8,128)(2,1)}, bf16[576,512]{1,0:T(8,128)(2,1)}, u32[]{:S(2)}, u32[]{:S(2)}) %collective-permute-start.1) | collective-permute-done | bytes 589856 | tf_op jit(solution)/shard_map/ppermute | solution.py:311
  68.9 6.6 %block_step.1 = (bf16[64,8,512]{2,1,0:T(8,128)(2,1)}, bf16[512,512]{1,0:T(8,128)(2,1)}, bf16[512,512]{1,0:T(8,128)(2,1)}, bf16[512,512]{1,0:T(8,128)(2,1)}) custom-call(s32[4]{0:T(128)S(1)} %add_convert_fusion.choice, bf16[64,8,512]{2,1,0:T(8,128)(2,1)S(1)} %all-to-all-done.1.shares_ref, bf16[2,512,512]{2,1,0:T(8,128)(2,1)S(1)} %copy-done.1, ...), custom_call_target="tpu_custom_call" | custom-call | flops 3221225472 | bytes 3145728 | tf_op jit(solution)/shard_map/block_step/pallas_call | solution.py:140
  75.5 15.3 %all-to-all-start.2 = ((bf16[64,8,512]{2,1,0:T(8,128)(2,1)}), bf16[64,8,512]{2,1,0:T(8,128)(2,1)S(1)}, u32[]{:S(2)}, u32[]{:S(2)}) async-start(bf16[64,8,512]{2,1,0:T(8,128)(2,1)} %get-tuple-element.9), calls=%async_computation.2 | async-start | bytes 1048576 | tf_op jit(solution)/shard_map/all_to_all | solution.py:366
  90.7 2.1 %collective-permute-start.2 = (bf16[512,512]{1,0:T(8,128)(2,1)}, bf16[512,512]{1,0:T(8,128)(2,1)}, u32[]{:S(2)}, u32[]{:S(2)}) collective-permute-start(bf16[512,512]{1,0:T(8,128)(2,1)} %get-tuple-element.10), channel_id=1, source_target_pairs={{0,256},{8,264},{16,272},{24,280},{32,288},{40,296},{48,304},{56,3... | collective-permute-start | bytes 1572872 | tf_op jit(solution)/shard_map/ppermute | solution.py:371
  92.9 21.5 %all-to-all-done.2.source = bf16[64,8,512]{2,1,0:T(8,128)(2,1)S(1)} async-done(((bf16[64,8,512]{2,1,0:T(8,128)(2,1)}), bf16[64,8,512]{2,1,0:T(8,128)(2,1)S(1)}, u32[]{:S(2)}, u32[]{:S(2)}) %all-to-all-start.2) | async-done | bytes 524320 | tf_op jit(solution)/shard_map/all_to_all | solution.py:366
  114.4 1.4 %reorder.4 = bf16[64,8,512]{2,1,0:T(8,128)(2,1)} custom-call(s32[64]{0:T(128)S(1)} %compare_select_fusion.9.order, bf16[64,8,512]{2,1,0:T(8,128)(2,1)S(1)} %all-to-all-done.2.source), custom_call_target="tpu_custom_call" | custom-call | tf_op jit(solution)/shard_map/reorder/pallas_call | solution.py:242
  115.8 5.5 %all-to-all-start.3 = ((bf16[64,8,512]{2,1,0:T(8,128)(2,1)}), bf16[64,8,512]{2,1,0:T(8,128)(2,1)S(1)}, u32[]{:S(2)}, u32[]{:S(2)}) async-start(bf16[64,8,512]{2,1,0:T(8,128)(2,1)} %reorder.4), calls=%async_computation.3 | async-start | bytes 1048576 | tf_op jit(solution)/shard_map/all_to_all | solution.py:375
  121.3 1.0 copy-done.3
  122.3 1.0 copy-done.4
  123.3 1.9 %settle_slots.1 = (bf16[2,512,512]{2,1,0:T(8,128)(2,1)}, bf16[2,512,512]{2,1,0:T(8,128)(2,1)}) custom-call(s32[4]{0:T(128)S(1)} %add_convert_fusion.choice, bf16[512,512]{1,0:T(8,128)(2,1)} %collective-permute-done.2.gradient_back, bf16[2,512,512]{2,1,0:T(8,128)(2,1)S(1)} %copy-done.1, bf16[2,512,512]{2,1,0:T(8,128)(2,1)S(1)} %copy-done.2, ...), custom_call_target="tpu_custom_call" | custom-call | flops 536870912 | bytes 4194304 | tf_op jit(solution)/shard_map/settle_slots/pallas_call | solution.py:214
  125.3 3.0 %all-to-all-done.3.source = bf16[64,8,512]{2,1,0:T(8,128)(2,1)S(1)} async-done(((bf16[64,8,512]{2,1,0:T(8,128)(2,1)}), bf16[64,8,512]{2,1,0:T(8,128)(2,1)S(1)}, u32[]{:S(2)}, u32[]{:S(2)}) %all-to-all-start.3) | async-done | bytes 524320 | tf_op jit(solution)/shard_map/all_to_all | solution.py:375
  128.3 1.4 %reorder.5 = bf16[64,8,512]{2,1,0:T(8,128)(2,1)} custom-call(s32[64]{0:T(128)S(1)} %fusion.15.order, bf16[64,8,512]{2,1,0:T(8,128)(2,1)S(1)} %all-to-all-done.3.source), custom_call_target="tpu_custom_call" | custom-call | tf_op jit(solution)/shard_map/reorder/pallas_call | solution.py:242
  (32 shorter events, 2.1 us)
Async XLA Ops:
  0.6 8.7 %copy-start = (bf16[64,8,512]{2,1,0:T(8,128)(2,1)S(1)}, bf16[64,8,512]{2,1,0:T(8,128)(2,1)}, u32[]{:S(2)}) copy-start(bf16[64,8,512]{2,1,0:T(8,128)(2,1)} %param.4) | copy-start | bytes 1572868
  2.5 16.5 %collective-permute-start = (bf16[448,512]{1,0:T(8,128)(2,1)}, bf16[448,512]{1,0:T(8,128)(2,1)}, u32[]{:S(2)}, u32[]{:S(2)}) collective-permute-start(bf16[448,512]{1,0:T(8,128)(2,1)} %slice_bitcast_fusion), channel_id=1, source_target_pairs={{0,256},{8,264},{16,272},{24,280},{32,288},{40,296},{48,304},{56,3... | collective-permute-start | bytes 1376264 | tf_op jit(solution)/shard_map/ppermute | solution.py:310
  8.2 0.7 copy-start.5
  10.7 14.3 %all-to-all-start = ((bf16[64,8,512]{2,1,0:T(8,128)(2,1)}), bf16[64,8,512]{2,1,0:T(8,128)(2,1)S(1)}, u32[]{:S(2)}, u32[]{:S(2)}) async-start(bf16[64,8,512]{2,1,0:T(8,128)(2,1)} %gather_fusion), calls=%async_computation | async-start | bytes 1048576 | tf_op jit(solution)/shard_map/all_to_all | solution.py:328
  19.0 26.0 %copy-start.1 = (bf16[2,512,512]{2,1,0:T(8,128)(2,1)S(1)}, bf16[2,512,512]{2,1,0:T(8,128)(2,1)}, u32[]{:S(2)}) copy-start(bf16[2,512,512]{2,1,0:T(8,128)(2,1)} %left_own.5) | copy-start | bytes 3145732
  19.0 26.0 %copy-start.2 = (bf16[2,512,512]{2,1,0:T(8,128)(2,1)S(1)}, bf16[2,512,512]{2,1,0:T(8,128)(2,1)}, u32[]{:S(2)}) copy-start(bf16[2,512,512]{2,1,0:T(8,128)(2,1)} %right_own.5) | copy-start | bytes 3145732
  26.4 42.4 %all-to-all-start.1 = ((bf16[64,8,512]{2,1,0:T(8,128)(2,1)}), bf16[64,8,512]{2,1,0:T(8,128)(2,1)S(1)}, u32[]{:S(2)}, u32[]{:S(2)}) async-start(bf16[64,8,512]{2,1,0:T(8,128)(2,1)} %reorder.3), calls=%async_computation.1 | async-start | bytes 1048576 | tf_op jit(solution)/shard_map/all_to_all | solution.py:351
  45.9 22.3 %collective-permute-start.1 = (bf16[576,512]{1,0:T(8,128)(2,1)}, bf16[576,512]{1,0:T(8,128)(2,1)}, u32[]{:S(2)}, u32[]{:S(2)}) collective-permute-start(bf16[576,512]{1,0:T(8,128)(2,1)} %late_loan.1), channel_id=1, source_target_pairs={{0,256},{8,264},{16,272},{24,280},{32,288},{40,296},{48,304},{56,3... | collective-permute-start | bytes 1769480 | tf_op jit(solution)/shard_map/ppermute | solution.py:311
  75.5 38.9 %all-to-all-start.2 = ((bf16[64,8,512]{2,1,0:T(8,128)(2,1)}), bf16[64,8,512]{2,1,0:T(8,128)(2,1)S(1)}, u32[]{:S(2)}, u32[]{:S(2)}) async-start(bf16[64,8,512]{2,1,0:T(8,128)(2,1)} %get-tuple-element.9), calls=%async_computation.2 | async-start | bytes 1048576 | tf_op jit(solution)/shard_map/all_to_all | solution.py:366
  90.7 30.5 %collective-permute-start.2 = (bf16[512,512]{1,0:T(8,128)(2,1)}, bf16[512,512]{1,0:T(8,128)(2,1)}, u32[]{:S(2)}, u32[]{:S(2)}) collective-permute-start(bf16[512,512]{1,0:T(8,128)(2,1)} %get-tuple-element.10), channel_id=1, source_target_pairs={{0,256},{8,264},{16,272},{24,280},{32,288},{40,296},{48,304},{56,3... | collective-permute-start | bytes 1572872 | tf_op jit(solution)/shard_map/ppermute | solution.py:371
  115.8 12.5 %all-to-all-start.3 = ((bf16[64,8,512]{2,1,0:T(8,128)(2,1)}), bf16[64,8,512]{2,1,0:T(8,128)(2,1)S(1)}, u32[]{:S(2)}, u32[]{:S(2)}) async-start(bf16[64,8,512]{2,1,0:T(8,128)(2,1)} %reorder.4), calls=%async_computation.3 | async-start | bytes 1048576 | tf_op jit(solution)/shard_map/all_to_all | solution.py:375
  121.3 1.0 copy-start.3
  122.3 1.0 copy-start.4
